TPU v7x, 256 devices: a whole 4x4x8 slice. The times are simulated.
256 devices in a mesh: blk: 8 (over x_lo, y), group: 32 (over x_hi, z, core).
Axes of the slice: x: 4 (x_hi: 2, x_lo: 2; x = x_hi * 2 + x_lo), y: 4, z: 8, core: 2. Of those that a mesh axis runs over, the one named last changes fastest.
Arguments:
- trace_emb: bfloat16 [131072, 1152], P(('blk', 'group')), may hold values from -1 to 1
- code_emb: bfloat16 [2048, 1152], P(('blk', 'group')), may hold values from -1 to 1
- trace_ids: int32 [131072], P(('blk', 'group')), may hold values from 0 to 511
- code_ids: int32 [2048], P(('blk', 'group')), may hold values from 0 to 511
- log_scale: float32 [1], replicated, may hold values from 3.9 to 4.2
- bias: float32 [1], replicated, may hold values from -7.5 to -6
Outputs:
- trace_grad: bfloat16 [131072, 1152], P(('blk', 'group'))
- code_grad: bfloat16 [2048, 1152], P(('blk', 'group'))
All inputs are finite; a program needn't handle non-finite values.
Results may differ from a plain program's by a relative error of at most 0.0044.
Values may be sent and summed in bfloat16 or wider, within the bound.
A program may use at most 128 MiB of HBM per device.

v0:
```python
import jax
import jax.numpy as jnp
from jax import lax
from jax.sharding import PartitionSpec as P


def passed_along(value, axis, steps):
    count = lax.axis_size(axis)
    pairs = [(source, (source + steps) % count) for source in range(count)]
    return lax.ppermute(value, axis, pairs)


def tile_slope(trace_emb, trace_ids, codes, code_labels, scale, shift):
    logits = (
        scale
        * lax.dot_general(
            trace_emb, codes, (((1,), (1,)), ((), ())), preferred_element_type=jnp.float32
        )
        + shift
    )
    sign = jnp.where(trace_ids[:, None] == code_labels[None, :], 1.0, -1.0).astype(jnp.float32)
    return (-scale * sign * jax.nn.sigmoid(-sign * logits)).astype(jnp.bfloat16)


def column_dot(slope, trace_emb):
    return lax.dot_general(
        slope, trace_emb, (((0,), (0,)), ((), ())), preferred_element_type=jnp.float32
    )


def per_device(trace_emb, code_emb, trace_ids, code_ids, log_scale, bias):
    scale = jnp.exp(log_scale[0])
    shift = bias[0]
    all_labels = lax.all_gather(code_ids, ("blk", "group"), axis=0, tiled=True)
    rows = trace_emb.shape[0]
    width = trace_emb.shape[1]
    blocks = lax.axis_size("blk")
    here = lax.axis_index("blk")
    visiting = lax.all_gather(code_emb, "group", axis=0, tiled=True)
    span = visiting.shape[0]
    trace_sum = jnp.zeros((rows, width), jnp.float32)
    carried = jnp.zeros((span, width), jnp.float32)
    for step in range(blocks):
        anchor = (here - step) % blocks
        labels = lax.dynamic_slice_in_dim(all_labels, anchor * span, span)
        slope = tile_slope(trace_emb, trace_ids, visiting, labels, scale, shift)
        trace_sum = trace_sum + jnp.dot(slope, visiting, preferred_element_type=jnp.float32)
        partial_sum = column_dot(slope, trace_emb)
        carried = passed_along(carried + partial_sum, "blk", 1)
        if step + 1 < blocks:
            visiting = passed_along(visiting, "blk", 1)
    code_sum = lax.psum_scatter(carried, "group", scatter_dimension=0, tiled=True)
    return (trace_sum.astype(jnp.bfloat16), code_sum.astype(jnp.bfloat16))


def solution(mesh):
    placed = (
        P(("blk", "group"), None),
        P(("blk", "group"), None),
        P(("blk", "group")),
        P(("blk", "group")),
        P(),
        P(),
    )
    return jax.shard_map(
        per_device,
        mesh=mesh,
        in_specs=placed,
        out_specs=(P(("blk", "group"), None), P(("blk", "group"), None)),
        check_vma=False,
    )
```

profile of v0, /device:TPU:16, one launch (start us, length us, event | category | flops | bytes accessed | tf_op | source)
XLA Modules:
  0.0 572.3 jit_solution(13556571107028383209)
XLA Ops:
  0.8 46.7 %all_gather.7 = bf16[256,1152]{1,0:T(8,128)(2,1)S(1)} all-gather(bf16[8,1152]{1,0:T(8,128)(2,1)} %param.7), channel_id=1, replica_groups=mesh['blk'=8,'group'=32] {'group'}, dimensions={0}, use_global_device_ids=true | all-gather | bytes 608256 | tf_op jit(solution)/shard_map/all_gather | solution.py:39
  49.7 72.9 %all-reduce = s32[2048]{0:T(1024)S(1)} all-reduce(s32[2048]{0:T(1024)S(1)} %dynamic-update-slice), channel_id=1, replica_groups=mesh['blk'=8,'group'=32] {'blk','group'}, use_global_device_ids=true, to_apply=%add | all-reduce | flops 2048 | bytes 16384
  128.4 36.7 %collective-permute-done = bf16[256,1152]{1,0:T(8,128)(2,1)S(1)} collective-permute-done((bf16[256,1152]{1,0:T(8,128)(2,1)S(1)}, bf16[256,1152]{1,0:T(8,128)(2,1)S(1)}, u32[]{:S(2)}, u32[]{:S(2)}) %collective-permute-start) | collective-permute-done | bytes 589856 | tf_op jit(solution)/shard_map/ppermute | solution.py:10
  168.6 3.6 collective-permute-start.1
  172.2 33.7 %collective-permute-done.1 = bf16[256,1152]{1,0:T(8,128)(2,1)S(1)} collective-permute-done((bf16[256,1152]{1,0:T(8,128)(2,1)S(1)}, bf16[256,1152]{1,0:T(8,128)(2,1)S(1)}, u32[]{:S(2)}, u32[]{:S(2)}) %collective-permute-start.1) | collective-permute-done | bytes 589856 | tf_op jit(solution)/shard_map/ppermute | solution.py:10
  210.5 4.6 collective-permute-start.2
  215.1 32.2 %collective-permute-done.2 = bf16[256,1152]{1,0:T(8,128)(2,1)S(1)} collective-permute-done((bf16[256,1152]{1,0:T(8,128)(2,1)S(1)}, bf16[256,1152]{1,0:T(8,128)(2,1)S(1)}, u32[]{:S(2)}, u32[]{:S(2)}) %collective-permute-start.2) | collective-permute-done | bytes 589856 | tf_op jit(solution)/shard_map/ppermute | solution.py:10
  248.8 3.9 collective-permute-start.10
  252.8 4.6 collective-permute-start.3
  257.3 31.4 %collective-permute-done.3 = bf16[256,1152]{1,0:T(8,128)(2,1)} collective-permute-done((bf16[256,1152]{1,0:T(8,128)(2,1)S(1)}, bf16[256,1152]{1,0:T(8,128)(2,1)}, u32[]{:S(2)}, u32[]{:S(2)}) %collective-permute-start.3) | collective-permute-done | bytes 589856 | tf_op jit(solution)/shard_map/ppermute | solution.py:10
  291.3 3.8 collective-permute-start.11
  295.1 4.7 collective-permute-start.4
  300.9 29.3 %collective-permute-done.4 = bf16[256,1152]{1,0:T(8,128)(2,1)} collective-permute-done((bf16[256,1152]{1,0:T(8,128)(2,1)}, bf16[256,1152]{1,0:T(8,128)(2,1)}, u32[]{:S(2)}, u32[]{:S(2)}) %collective-permute-start.4) | collective-permute-done | bytes 589856 | tf_op jit(solution)/shard_map/ppermute | solution.py:10
  330.2 3.9 collective-permute-start.5
  337.8 4.7 collective-permute-start.12
  343.5 4.7 collective-permute-done.5
  348.3 4.6 collective-permute-start.6
  354.0 19.5 %collective-permute-done.12 = f32[256,1152]{1,0:T(8,128)S(1)} collective-permute-done((f32[256,1152]{1,0:T(8,128)S(1)}, f32[256,1152]{1,0:T(8,128)S(1)}, u32[]{:S(2)}, u32[]{:S(2)}) %collective-permute-start.12) | collective-permute-done | bytes 1179680 | tf_op jit(solution)/shard_map/ppermute | solution.py:10
  373.7 4.5 collective-permute-start.13
  379.3 6.9 %collective-permute-done.6 = bf16[256,1152]{1,0:T(8,128)(2,1)S(1)} collective-permute-done((bf16[256,1152]{1,0:T(8,128)(2,1)S(1)}, bf16[256,1152]{1,0:T(8,128)(2,1)S(1)}, u32[]{:S(2)}, u32[]{:S(2)}) %collective-permute-start.6) | collective-permute-done | bytes 589856 | tf_op jit(solution)/shard_map/ppermute | solution.py:10
  387.4 19.6 %collective-permute-done.13 = f32[256,1152]{1,0:T(8,128)S(1)} collective-permute-done((f32[256,1152]{1,0:T(8,128)S(1)}, f32[256,1152]{1,0:T(8,128)S(1)}, u32[]{:S(2)}, u32[]{:S(2)}) %collective-permute-start.13) | collective-permute-done | bytes 1179680 | tf_op jit(solution)/shard_map/ppermute | solution.py:10
  407.1 4.0 collective-permute-start.14
  416.3 15.2 %collective-permute-done.14 = f32[256,1152]{1,0:T(8,128)S(1)} collective-permute-done((f32[256,1152]{1,0:T(8,128)S(1)}, f32[256,1152]{1,0:T(8,128)S(1)}, u32[]{:S(2)}, u32[]{:S(2)}) %collective-permute-start.14) | collective-permute-done | bytes 1179680 | tf_op jit(solution)/shard_map/ppermute | solution.py:10
  431.5 140.2 %all-reduce.3 = bf16[256,1152]{1,0:T(8,128)(2,1)S(1)} all-reduce(f32[256,1152]{1,0:T(8,128)S(1)} %collective-permute-done.14), channel_id=2, replica_groups=mesh['blk'=8,'group'=32] {'group'}, use_global_device_ids=true, to_apply=%region_0.1.clone | all-reduce | flops 294912 | bytes 1769472
  (74 shorter events, 33.3 us)
Async XLA Ops:
  0.6 122.1 %copy-start = (bf16[512,1152]{1,0:T(8,128)(2,1)S(1)}, bf16[512,1152]{1,0:T(8,128)(2,1)}, u32[]{:S(2)}) copy-start(bf16[512,1152]{1,0:T(8,128)(2,1)} %param.6) | copy-start | bytes 3538948
  124.0 41.0 %copy-start.13 = (s32[512]{0:T(512)S(1)}, s32[512]{0:T(512)}, u32[]{:S(2)}) copy-start(s32[512]{0:T(512)} %param.8) | copy-start | bytes 6148
  124.6 41.1 %collective-permute-start.7 = (f32[256,1152]{1,0:T(8,128)S(1)}, f32[256,1152]{1,0:T(8,128)S(1)}, u32[]{:S(2)}, u32[]{:S(2)}) collective-permute-start(f32[256,1152]{1,0:T(8,128)S(1)} %fusion.67), channel_id=1, source_target_pairs={{0,32},{32,64},{64,96},{96,128},{128,160},{160,192},{192,224},{224... | collective-permute-start | bytes 3538952 | tf_op jit(solution)/shard_map/ppermute | solution.py:10
  126.9 38.2 %collective-permute-start = (bf16[256,1152]{1,0:T(8,128)(2,1)S(1)}, bf16[256,1152]{1,0:T(8,128)(2,1)S(1)}, u32[]{:S(2)}, u32[]{:S(2)}) collective-permute-start(bf16[256,1152]{1,0:T(8,128)(2,1)S(1)} %all_gather.7), channel_id=1, source_target_pairs={{0,32},{32,64},{64,96},{96,128},{128,160},{160,192},{192,224},{224... | collective-permute-start | bytes 1769480 | tf_op jit(solution)/shard_map/ppermute | solution.py:10
  166.4 40.7 %collective-permute-start.8 = (f32[256,1152]{1,0:T(8,128)S(1)}, f32[256,1152]{1,0:T(8,128)S(1)}, u32[]{:S(2)}, u32[]{:S(2)}) collective-permute-start(f32[256,1152]{1,0:T(8,128)S(1)} %convolution_add_fusion.7), channel_id=1, source_target_pairs={{0,32},{32,64},{64,96},{96,128},{128,160},{160,192},{192,224},{224... | collective-permute-start | bytes 3538952 | tf_op jit(solution)/shard_map/ppermute | solution.py:10
  168.6 37.3 %collective-permute-start.1 = (bf16[256,1152]{1,0:T(8,128)(2,1)S(1)}, bf16[256,1152]{1,0:T(8,128)(2,1)S(1)}, u32[]{:S(2)}, u32[]{:S(2)}) collective-permute-start(bf16[256,1152]{1,0:T(8,128)(2,1)S(1)} %collective-permute-done), channel_id=1, source_target_pairs={{0,32},{32,64},{64,96},{96,128},{128,160},{160,192},{192,224},{224... | collective-permute-start | bytes 1769480 | tf_op jit(solution)/shard_map/ppermute | solution.py:10
  207.2 41.5 %collective-permute-start.9 = (f32[256,1152]{1,0:T(8,128)S(1)}, f32[256,1152]{1,0:T(8,128)S(1)}, u32[]{:S(2)}, u32[]{:S(2)}) collective-permute-start(f32[256,1152]{1,0:T(8,128)S(1)} %add.199), channel_id=1, source_target_pairs={{0,32},{32,64},{64,96},{96,128},{128,160},{160,192},{192,224},{224... | collective-permute-start | bytes 3538952 | tf_op jit(solution)/shard_map/ppermute | solution.py:10
  210.5 36.8 %collective-permute-start.2 = (bf16[256,1152]{1,0:T(8,128)(2,1)S(1)}, bf16[256,1152]{1,0:T(8,128)(2,1)S(1)}, u32[]{:S(2)}, u32[]{:S(2)}) collective-permute-start(bf16[256,1152]{1,0:T(8,128)(2,1)S(1)} %collective-permute-done.1), channel_id=1, source_target_pairs={{0,32},{32,64},{64,96},{96,128},{128,160},{160,192},{192,224},{224... | collective-permute-start | bytes 1769480 | tf_op jit(solution)/shard_map/ppermute | solution.py:10
  247.4 5.4 copy-start.11
  248.8 42.3 %collective-permute-start.10 = (f32[256,1152]{1,0:T(8,128)S(1)}, f32[256,1152]{1,0:T(8,128)S(1)}, u32[]{:S(2)}, u32[]{:S(2)}) collective-permute-start(f32[256,1152]{1,0:T(8,128)S(1)} %add.200), channel_id=1, source_target_pairs={{0,32},{32,64},{64,96},{96,128},{128,160},{160,192},{192,224},{224... | collective-permute-start | bytes 3538952 | tf_op jit(solution)/shard_map/ppermute | solution.py:10
  252.8 36.0 %collective-permute-start.3 = (bf16[256,1152]{1,0:T(8,128)(2,1)S(1)}, bf16[256,1152]{1,0:T(8,128)(2,1)}, u32[]{:S(2)}, u32[]{:S(2)}) collective-permute-start(bf16[256,1152]{1,0:T(8,128)(2,1)S(1)} %collective-permute-done.2), channel_id=1, source_target_pairs={{0,32},{32,64},{64,96},{96,128},{128,160},{160,192},{192,224},{224... | collective-permute-start | bytes 1769480 | tf_op jit(solution)/shard_map/ppermute | solution.py:10
  291.1 8.7 %copy-start.14 = (u32[256]{0:T(256)S(1)}, u32[256]{0:T(256)}, u32[]{:S(2)}) copy-start(u32[256]{0:T(256)} %constant.86) | copy-start | bytes 3076
  291.3 45.2 %collective-permute-start.11 = (f32[256,1152]{1,0:T(8,128)S(1)}, f32[256,1152]{1,0:T(8,128)}, u32[]{:S(2)}, u32[]{:S(2)}) collective-permute-start(f32[256,1152]{1,0:T(8,128)S(1)} %add.201), channel_id=1, source_target_pairs={{0,32},{32,64},{64,96},{96,128},{128,160},{160,192},{192,224},{224... | collective-permute-start | bytes 3538952 | tf_op jit(solution)/shard_map/ppermute | solution.py:10
  295.1 35.1 %collective-permute-start.4 = (bf16[256,1152]{1,0:T(8,128)(2,1)}, bf16[256,1152]{1,0:T(8,128)(2,1)}, u32[]{:S(2)}, u32[]{:S(2)}) collective-permute-start(bf16[256,1152]{1,0:T(8,128)(2,1)} %collective-permute-done.3), channel_id=1, source_target_pairs={{0,32},{32,64},{64,96},{96,128},{128,160},{160,192},{192,224},{224... | collective-permute-start | bytes 1769480 | tf_op jit(solution)/shard_map/ppermute | solution.py:10
  330.2 18.0 %collective-permute-start.5 = (bf16[256,1152]{1,0:T(8,128)(2,1)}, bf16[256,1152]{1,0:T(8,128)(2,1)S(1)}, u32[]{:S(2)}, u32[]{:S(2)}) collective-permute-start(bf16[256,1152]{1,0:T(8,128)(2,1)} %collective-permute-done.4), channel_id=1, source_target_pairs={{0,32},{32,64},{64,96},{96,128},{128,160},{160,192},{192,224},{224... | collective-permute-start | bytes 1769480 | tf_op jit(solution)/shard_map/ppermute | solution.py:10
  337.8 5.2 copy-start.6
  337.8 5.2 copy-start.10
  337.8 35.7 %collective-permute-start.12 = (f32[256,1152]{1,0:T(8,128)S(1)}, f32[256,1152]{1,0:T(8,128)S(1)}, u32[]{:S(2)}, u32[]{:S(2)}) collective-permute-start(f32[256,1152]{1,0:T(8,128)S(1)} %add.202), channel_id=1, source_target_pairs={{0,32},{32,64},{64,96},{96,128},{128,160},{160,192},{192,224},{224... | collective-permute-start | bytes 3538952 | tf_op jit(solution)/shard_map/ppermute | solution.py:10
  348.3 37.9 %collective-permute-start.6 = (bf16[256,1152]{1,0:T(8,128)(2,1)S(1)}, bf16[256,1152]{1,0:T(8,128)(2,1)S(1)}, u32[]{:S(2)}, u32[]{:S(2)}) collective-permute-start(bf16[256,1152]{1,0:T(8,128)(2,1)S(1)} %collective-permute-done.5), channel_id=1, source_target_pairs={{0,32},{32,64},{64,96},{96,128},{128,160},{160,192},{192,224},{224... | collective-permute-start | bytes 1769480 | tf_op jit(solution)/shard_map/ppermute | solution.py:10
  354.0 24.2 %copy-start.8 = (bf16[256,1152]{1,0:T(8,128)(2,1)S(1)}, bf16[256,1152]{1,0:T(8,128)(2,1)}, u32[]{:S(2)}) copy-start(bf16[256,1152]{1,0:T(8,128)(2,1)} %copy-done.7) | copy-start | bytes 1769476
  373.7 5.1 copy-start.4
  373.7 33.2 %collective-permute-start.13 = (f32[256,1152]{1,0:T(8,128)S(1)}, f32[256,1152]{1,0:T(8,128)S(1)}, u32[]{:S(2)}, u32[]{:S(2)}) collective-permute-start(f32[256,1152]{1,0:T(8,128)S(1)} %add.203), channel_id=1, source_target_pairs={{0,32},{32,64},{64,96},{96,128},{128,160},{160,192},{192,224},{224... | collective-permute-start | bytes 3538952 | tf_op jit(solution)/shard_map/ppermute | solution.py:10
  387.3 23.7 %copy-start.2 = (bf16[512,256]{1,0:T(8,128)(2,1)S(1)}, bf16[512,256]{1,0:T(8,128)(2,1)}, u32[]{:S(2)}) copy-start(bf16[512,256]{1,0:T(8,128)(2,1)} %copy-done.1) | copy-start | bytes 786436
  407.1 24.5 %collective-permute-start.14 = (f32[256,1152]{1,0:T(8,128)S(1)}, f32[256,1152]{1,0:T(8,128)S(1)}, u32[]{:S(2)}, u32[]{:S(2)}) collective-permute-start(f32[256,1152]{1,0:T(8,128)S(1)} %add.204), channel_id=1, source_target_pairs={{0,32},{32,64},{64,96},{96,128},{128,160},{160,192},{192,224},{224... | collective-permute-start | bytes 3538952 | tf_op jit(solution)/shard_map/ppermute | solution.py:10
  (6 other events, 15.3 us)
where the time goes:
time: 579 us; the launch traced here: 572 us
  blocking collectives  260 us (45%)
  waiting for transfers between devices  229 us (40%)
  starting transfers between devices  56.2 us (10%)
  matrix products  19.3 us (3%)
    ppermute x15, waiting for transfers between devices, passed_along(): return lax.ppermute(value, axis, pairs)  229 us
    unnamed x2, blocking collectives  213 us
    ppermute x15, starting transfers between devices, passed_along(): return lax.ppermute(value, axis, pairs)  56.2 us
    all_gather x1, blocking collectives, per_device(): visiting = lax.all_gather(code_emb, 'group', axis=0, tiled=True)  46.7 us
  transfers between devices with their start and end apart: 15, of which 10 were waited for; matrix products, arithmetic and copies ran while one was open for 3% of the time, Pallas kernels for 0%

commit v1 on v0

v1 whole, which is shorter than its diff:
```python
import jax
import jax.numpy as jnp
from jax import lax
from jax.experimental import pallas as pl
from jax.experimental.pallas import tpu as pltpu
from jax.sharding import PartitionSpec as P

MESH = pl.DeviceIdType.MESH
F32 = jnp.float32
BF16 = jnp.bfloat16

NY, NX, NZ = 4, 4, 8
SHARD = 8
WIDTH = 1152
ROWS = 512
A0, A1 = 0, 512
B0, B1 = 512, 1024
C0, C1 = 1024, 1152
WIDE = 1280
SPAN = NX * NZ * SHARD
PLANE = NY * SPAN


def place():
    blk = lax.axis_index("blk")
    group = lax.axis_index("group")
    x = (group // 16) * 2 + blk // 4
    return blk % 4, x, (group // 2) % NZ, group % 2


def device(y, x, z, core):
    return ((x % 2) * 4 + y, ((x // 2) * NZ + z) * 2 + core)


def remote(src, dst, sems, index, target):
    return pltpu.make_async_remote_copy(
        src_ref=src,
        dst_ref=dst,
        send_sem=sems[0].at[index],
        recv_sem=sems[1].at[index],
        device_id=target,
        device_id_type=MESH,
    )


def kernel(
    trace_ref, code_ref, tid_ref, cid_ref, scale_ref, shift_ref,
    trace_out, code_out,
    traces, tids, codes, flat, slopes, parts,
    recv_a1, recv_b1, recv_c1, sum_a, sum_b, sum_c, recv_a2, recv_b2, recv_c2,
    sum_ab, sum_c2, recv_ab3, recv_c3, tg_own, tg_send, tg_recv,
    s_d, r_d, s_ag, r_ag, s_rs, r_rs,
):
    y, x, z, core = place()
    ag = (s_ag, r_ag)
    rs = (s_rs, r_rs)
    dd = (s_d, r_d)

    def on_y(k):
        return device((y + k) % NY, x, z, core)

    def on_x(k):
        return device(y, (x + k) % NX, z, core)

    def on_z(k):
        return device(y, x, (z + k) % NZ, core)

    other = device(y, x, z, 1 - core)

    barrier = pltpu.get_barrier_semaphore()
    partners = [on_y(k) for k in (1, 2, 3)] + [on_x(k) for k in (1, 2, 3)]
    partners += [on_z(k) for k in range(1, NZ)] + [other]
    for partner in partners:
        pl.semaphore_signal(barrier, inc=1, device_id=partner, device_id_type=MESH)

    ids = cid_ref[...].astype(jnp.int32)
    high = (ids // 16).astype(F32)
    low = (ids % 16).astype(F32)
    lane = lax.broadcasted_iota(jnp.int32, (SHARD, 128), 1)
    tile = jnp.where(lane == 0, high, jnp.where(lane == 1, low, 0.0)).astype(BF16)
    codes[y, x, z, :, 0:WIDTH] = code_ref[...]
    codes[y, x, z, :, WIDTH:WIDE] = tile
    pl.semaphore_wait(barrier, len(partners))

    g1 = []
    for k in range(1, NZ):
        ref = codes.at[y, x, z, :, A0:B1]
        g1.append(remote(ref, ref, ag, k - 1, on_z(k)))
    g1c = []
    for k in range(1, NX):
        ref = codes.at[y, x, z, :, C0:WIDE]
        g1c.append(remote(ref, ref, ag, 6 + k, on_x(k)))
    for copy in g1 + g1c:
        copy.start()

    d1 = remote(trace_ref, traces.at[ROWS : 2 * ROWS], dd, 0, other)
    d2 = remote(tid_ref, tids.at[1], dd, 1, other)
    d1.start()
    d2.start()
    traces[0:ROWS] = trace_ref[...]
    tids[0] = tid_ref[...]

    g2 = []
    for copy in g1c:
        copy.wait_recv()
    for k in range(1, NY):
        ref = codes.at[y, :, z, :, C0:WIDE]
        g2.append(remote(ref, ref, ag, 9 + k, on_y(k)))
        g2[-1].start()
    g2c = list(g2)
    for copy in g1:
        copy.wait_recv()
    g2ab = []
    for k in range(1, 4):
        ref = codes.at[y, x, :, :, A0:A1]
        g2ab.append(remote(ref, ref, ag, 12 + k, on_x(k)))
        ref = codes.at[y, x, :, :, B0:B1]
        g2ab.append(remote(ref, ref, ag, 15 + k, on_y(k)))
    for copy in g2ab:
        copy.start()

    g3 = []
    for copy in g2c:
        copy.wait_recv()
    for k in range(1, NZ):
        ref = codes.at[:, :, z, :, C0:WIDE]
        g3.append(remote(ref, ref, ag, 18 + k, on_z(k)))
        g3[-1].start()
    for copy in g2ab:
        copy.wait_recv()
    for k in range(1, 4):
        ref = codes.at[y, :, :, :, A0:A1]
        g3.append(remote(ref, ref, ag, 25 + k, on_y(k)))
        g3[-1].start()
        ref = codes.at[:, x, :, :, B0:B1]
        g3.append(remote(ref, ref, ag, 28 + k, on_x(k)))
        g3[-1].start()
    d1.wait()
    d2.wait()
    for copy in g3:
        copy.wait_recv()

    scale = jnp.exp(scale_ref[...])
    shift = shift_ref[...]
    trace_ids = jnp.concatenate([tids[0], tids[1]], axis=1).astype(F32)

    def send_a1(j, q):
        return remote(
            parts.at[q, :, :, :, A0:A1], recv_a1.at[j - 1], rs, j - 1, on_y(j)
        )

    def send_b1(j, q, k):
        return remote(
            parts.at[q, (x + k) % NX, :, :, B0:B1], recv_b1.at[k - 1, q], rs, 3 + j * 3 + k - 1, on_x(k)
        )

    @pl.loop(0, NY)
    def _(step):
        j = (step + 1) % NY
        q = (y + j) % NY
        at = pl.multiple_of(q * SPAN, SPAN)
        for i in range(NX):
            block = codes[q, i, :, :, 0:WIDTH].astype(F32).reshape(NZ * SHARD, WIDTH)
            flat[pl.ds(at + i * NZ * SHARD, NZ * SHARD), :] = block.astype(BF16)
        marks = codes[q, :, :, :, WIDTH:WIDE].astype(F32).reshape(SPAN, 128)
        code_ids = marks[:, 0:1] * 16.0 + marks[:, 1:2]
        logits = lax.dot_general(
            flat[pl.ds(at, SPAN), :], traces[...], (((1,), (1,)), ((), ())), preferred_element_type=F32
        )
        logits = logits * scale + shift
        same = code_ids == trace_ids
        raised = jnp.exp(jnp.where(same, logits, -logits))
        slope = jnp.where(same, -scale, scale) / (1.0 + raised)
        slopes[pl.ds(at, SPAN), :] = slope.astype(BF16)
        grad = jnp.dot(slopes[pl.ds(at, SPAN), :], traces[...], preferred_element_type=F32)
        parts[q] = grad.reshape(NX, NZ, SHARD, WIDTH).astype(BF16)

        @pl.when(j != 0)
        def _():
            send_a1(j, q).start()

        for k in range(1, NX):
            send_b1(j, q, k).start()

    c1 = []
    for k in range(1, NZ):
        c1.append(
            remote(parts.at[:, :, (z + k) % NZ, :, C0:C1], recv_c1.at[k - 1], rs, 14 + k, on_z(k))
        )
        c1[-1].start()

    def trace_rows(first):
        return lax.dot_general(
            slopes[:, first : first + 256], flat[...], (((0,), (0,)), ((), ())), preferred_element_type=F32
        )

    for n in range(2):
        tg_send[n * 256 : n * 256 + 256, :] = trace_rows(ROWS + n * 256)
    d3 = remote(tg_send, tg_recv, dd, 2, other)
    d3.start()
    for n in range(2):
        tg_own[n * 256 : n * 256 + 256, :] = trace_rows(n * 256)

    for copy in c1:
        copy.wait_recv()
    for i in range(NY):
        total = parts[i, :, z, :, C0:C1].astype(F32)
        for k in range(NZ - 1):
            total = total + recv_c1[k, i].astype(F32)
        sum_c[i] = total.astype(BF16)
    c2 = []
    for k in range(1, NY):
        c2.append(remote(sum_c.at[(y + k) % NY], recv_c2.at[k - 1], rs, 21 + k, on_y(k)))
        c2[-1].start()

    for k in range(1, NX):
        for j in range(NY):
            send_b1(j, (y + j) % NY, k).wait_recv()
    for i in range(NY):
        total = parts[i, x, :, :, B0:B1].astype(F32)
        for k in range(NX - 1):
            total = total + recv_b1[k, i].astype(F32)
        sum_b[i] = total.astype(BF16)
    b2 = []
    for k in range(1, NY):
        b2.append(remote(sum_b.at[(y + k) % NY], recv_b2.at[k - 1], rs, 24 + k, on_y(k)))
        b2[-1].start()

    for j in range(1, NY):
        send_a1(j, (y + j) % NY).wait_recv()
    for i in range(NX):
        total = parts[y, i, :, :, A0:A1].astype(F32)
        for k in range(NY - 1):
            total = total + recv_a1[k, i].astype(F32)
        sum_a[i] = total.astype(BF16)
    a2 = []
    for k in range(1, NX):
        a2.append(remote(sum_a.at[(x + k) % NX], recv_a2.at[k - 1], rs, 27 + k, on_x(k)))
        a2[-1].start()

    for copy in c2:
        copy.wait_recv()
    total = sum_c[y].astype(F32)
    for k in range(NY - 1):
        total = total + recv_c2[k].astype(F32)
    sum_c2[...] = total.astype(BF16)
    c3 = []
    for k in range(1, NX):
        c3.append(remote(sum_c2.at[(x + k) % NX], recv_c3.at[k - 1], rs, 30 + k, on_x(k)))
        c3[-1].start()
    for copy in b2:
        copy.wait_recv()
    total = sum_b[y].astype(F32)
    for k in range(NY - 1):
        total = total + recv_b2[k].astype(F32)
    sum_ab[:, :, B0:B1] = total.astype(BF16)
    for copy in a2:
        copy.wait_recv()
    total = sum_a[x].astype(F32)
    for k in range(NX - 1):
        total = total + recv_a2[k].astype(F32)
    sum_ab[:, :, A0:A1] = total.astype(BF16)
    ab3 = []
    for k in range(1, NZ):
        ab3.append(remote(sum_ab.at[(z + k) % NZ], recv_ab3.at[k - 1], rs, 33 + k, on_z(k)))
        ab3[-1].start()

    d3.wait()
    trace_out[...] = (tg_own[...] + tg_recv[...]).astype(BF16)

    for copy in c3:
        copy.wait_recv()
    total = sum_c2[x].astype(F32)
    for k in range(NX - 1):
        total = total + recv_c3[k].astype(F32)
    code_out[:, C0:C1] = total.astype(BF16)
    for copy in ab3:
        copy.wait_recv()
    total = sum_ab[z].astype(F32)
    for k in range(NZ - 1):
        total = total + recv_ab3[k].astype(F32)
    code_out[:, A0:B1] = total.astype(BF16)

    for copy in g1 + g1c + g2c + g2ab + g3 + c1 + c2 + b2 + a2 + c3 + ab3:
        copy.wait_send()
    for j in range(NY):
        if j:
            send_a1(j, (y + j) % NY).wait_send()
        for k in range(1, NX):
            send_b1(j, (y + j) % NY, k).wait_send()


def per_device(trace_emb, code_emb, trace_ids, code_ids, log_scale, bias):
    vmem = pl.BlockSpec(memory_space=pltpu.VMEM)
    dma = pltpu.SemaphoreType.DMA
    scratch = [
        pltpu.VMEM((2 * ROWS, WIDTH), BF16),
        pltpu.VMEM((2, 1, ROWS), jnp.int32),
        pltpu.VMEM((NY, NX, NZ, SHARD, WIDE), BF16),
        pltpu.VMEM((PLANE, WIDTH), BF16),
        pltpu.VMEM((PLANE, 2 * ROWS), BF16),
        pltpu.VMEM((NY, NX, NZ, SHARD, WIDTH), BF16),
        pltpu.VMEM((NY - 1, NX, NZ, SHARD, A1 - A0), BF16),
        pltpu.VMEM((NX - 1, NY, NZ, SHARD, B1 - B0), BF16),
        pltpu.VMEM((NZ - 1, NY, NX, SHARD, C1 - C0), BF16),
        pltpu.VMEM((NX, NZ, SHARD, A1 - A0), BF16),
        pltpu.VMEM((NY, NZ, SHARD, B1 - B0), BF16),
        pltpu.VMEM((NY, NX, SHARD, C1 - C0), BF16),
        pltpu.VMEM((NX - 1, NZ, SHARD, A1 - A0), BF16),
        pltpu.VMEM((NY - 1, NZ, SHARD, B1 - B0), BF16),
        pltpu.VMEM((NY - 1, NX, SHARD, C1 - C0), BF16),
        pltpu.VMEM((NZ, SHARD, B1 - A0), BF16),
        pltpu.VMEM((NX, SHARD, C1 - C0), BF16),
        pltpu.VMEM((NZ - 1, SHARD, B1 - A0), BF16),
        pltpu.VMEM((NX - 1, SHARD, C1 - C0), BF16),
        pltpu.VMEM((ROWS, WIDTH), F32),
        pltpu.VMEM((ROWS, WIDTH), F32),
        pltpu.VMEM((ROWS, WIDTH), F32),
        dma((3,)),
        dma((3,)),
        dma((32,)),
        dma((32,)),
        dma((41,)),
        dma((41,)),
    ]
    return pl.pallas_call(
        kernel,
        out_shape=(
            jax.ShapeDtypeStruct((ROWS, WIDTH), BF16),
            jax.ShapeDtypeStruct((SHARD, WIDTH), BF16),
        ),
        in_specs=[vmem] * 6,
        out_specs=(vmem, vmem),
        scratch_shapes=scratch,
        compiler_params=pltpu.CompilerParams(
            collective_id=0, has_side_effects=True, vmem_limit_bytes=56 * 2**20
        ),
        name="contrast",
    )(
        trace_emb,
        code_emb,
        trace_ids.reshape(1, ROWS),
        code_ids.reshape(SHARD, 1),
        log_scale.reshape(1, 1),
        bias.reshape(1, 1),
    )


def solution(mesh):
    placed = (
        P(("blk", "group"), None),
        P(("blk", "group"), None),
        P(("blk", "group")),
        P(("blk", "group")),
        P(),
        P(),
    )
    return jax.shard_map(
        per_device,
        mesh=mesh,
        in_specs=placed,
        out_specs=(P(("blk", "group"), None), P(("blk", "group"), None)),
        check_vma=False,
    )
```

time: 579 us -> 69.4 us (0.12); the launches traced: 572 us -> 68.8 us
  blocking collectives: 260 us -> 0 us
  waiting for transfers between devices: 229 us -> 0 us
  Pallas kernels: 0 us -> 62.5 us
  starting transfers between devices: 56.2 us -> 0 us
  matrix products: 19.3 us -> 0 us
    ppermute x15 -> x0, waiting for transfers between devices: 229 us -> none  [passed_along(): return lax.ppermute(value, axis, pairs)]
    unnamed x2 -> x0, blocking collectives: 213 us -> none
    pallas_call x0 -> x1, Pallas kernels: none -> 62.5 us  [per_device(): pl.pallas_call(kernel, out_shape=(jax.ShapeDtypeStruct((ROWS, WIDTH), BF1...]
    ppermute x15 -> x0, starting transfers between devices: 56.2 us -> none  [passed_along(): return lax.ppermute(value, axis, pairs)]
    all_gather x1 -> x0, blocking collectives: 46.7 us -> none  [per_device(): visiting = lax.all_gather(code_emb, 'group', axis=0, tiled=True)]
    dot_general x24 -> x0, matrix products: 19.3 us -> none  [the longest x8 7.83 us: tile_slope(): lax.dot_general(trace_emb, codes, (((1,), (1,)), ((), ())), preferred_ele...]
  transfers between devices with their start and end apart: 15 -> 0, of which waited for: 10 -> 0; matrix products, arithmetic and copies ran while one was open for 3% -> 0% of each run, Pallas kernels for 0% -> 0%
where the time goes in v1:
time: 69.4 us; the launch traced here: 68.8 us
  Pallas kernels  62.5 us (90%)
  local copies, waits for them, and re-layouts  4.31 us (6%)
  between operations  1.94 us (3%)
    pallas_call x1, Pallas kernels, per_device(): pl.pallas_call(kernel, out_shape=(jax.ShapeDtypeStruct((ROWS, WIDTH), BF1...  62.5 us
    unnamed x4, local copies, waits for them, and re-layouts  2.99 us

profile of v1, /device:TPU:16, one launch (start us, length us, event | category | flops | bytes accessed | tf_op | source)
XLA Modules:
  0.0 68.8 jit_solution(13986990444134583496)
XLA Ops:
  1.9 1.3 %copy.8.cid_ref = s32[8,1]{1,0:T(8,128)} copy(s32[8,1]{0,1:T(1,128)} %bitcast.7) | data formatting | bytes 64 | tf_op jit(solution)/shard_map/reshape | solution.py:343
  3.2 62.5 %contrast.1 = (bf16[512,1152]{1,0:T(8,128)(2,1)}, bf16[8,1152]{1,0:T(8,128)(2,1)}) custom-call(bf16[512,1152]{1,0:T(8,128)(2,1)} %trace_ref.1, bf16[8,1152]{1,0:T(8,128)(2,1)} %code_ref.1, s32[1,512]{1,0:T(1,128)} %bitcast.6, s32[8,1]{1,0:T(8,128)} %copy.8.cid_ref, f32[1,1]{1,0:T(1,128)} %bitcast.4.scale_ref, f32[1,1]{1,0:T(1,128)} %bitcast.5.shift_ref), custom_call_target="tpu_custom_call" | custom-call | tf_op jit(solution)/shard_map/contrast/pallas_call | solution.py:326
  65.8 0.0 copy-start
  65.8 2.4 %copy.13 = bf16[512,1152]{1,0:T(8,128)(2,1)} copy(bf16[512,1152]{1,0:T(8,128)(2,1)} %get-tuple-element.4) | data formatting | bytes 2359296
  68.2 0.0 copy-done
  68.2 0.6 copy.14
Async XLA Ops:
  65.8 2.4 %copy-start = (bf16[8,1152]{1,0:T(8,128)(2,1)S(1)}, bf16[8,1152]{1,0:T(8,128)(2,1)}, u32[]{:S(2)}) copy-start(bf16[8,1152]{1,0:T(8,128)(2,1)} %get-tuple-element.5) | copy-start | bytes 55300

commit v2 on v1

--- a/solution.py
+++ b/solution.py
@@ -49,12 +49,13 @@
     traces, tids, codes, flat, slopes, parts,
     recv_a1, recv_b1, recv_c1, sum_a, sum_b, sum_c, recv_a2, recv_b2, recv_c2,
     sum_ab, sum_c2, recv_ab3, recv_c3, tg_own, tg_send, tg_recv,
-    s_d, r_d, s_ag, r_ag, s_rs, r_rs,
+    local, s_d, r_d, s_ag, r_ag, s_g3a, r_g3a, s_g3b, r_g3b, s_g3c, r_g3c, s_rs, r_rs,
 ):
     y, x, z, core = place()
     ag = (s_ag, r_ag)
     rs = (s_rs, r_rs)
     dd = (s_d, r_d)
+    g3a, g3b, g3c = (s_g3a, r_g3a), (s_g3b, r_g3b), (s_g3c, r_g3c)
 
     def on_y(k):
         return device((y + k) % NY, x, z, core)
@@ -73,7 +74,10 @@
     for partner in partners:
         pl.semaphore_signal(barrier, inc=1, device_id=partner, device_id_type=MESH)
 
-    ids = cid_ref[...].astype(jnp.int32)
+    spread = jnp.broadcast_to(cid_ref[...], (SHARD, SHARD))
+    row = lax.broadcasted_iota(jnp.int32, (SHARD, SHARD), 0)
+    column = lax.broadcasted_iota(jnp.int32, (SHARD, SHARD), 1)
+    ids = jnp.sum(jnp.where(row == column, spread, 0), axis=1, keepdims=True)
     high = (ids // 16).astype(F32)
     low = (ids % 16).astype(F32)
     lane = lax.broadcasted_iota(jnp.int32, (SHARD, 128), 1)
@@ -82,63 +86,69 @@
     codes[y, x, z, :, WIDTH:WIDE] = tile
     pl.semaphore_wait(barrier, len(partners))
 
-    g1 = []
-    for k in range(1, NZ):
-        ref = codes.at[y, x, z, :, A0:B1]
-        g1.append(remote(ref, ref, ag, k - 1, on_z(k)))
-    g1c = []
-    for k in range(1, NX):
-        ref = codes.at[y, x, z, :, C0:WIDE]
-        g1c.append(remote(ref, ref, ag, 6 + k, on_x(k)))
-    for copy in g1 + g1c:
+    near_z = (1, 7, 2, 6, 3, 5, 4)
+    near = (1, 3, 2)
+    sent = []
+
+    def go(copy):
         copy.start()
-
+        sent.append(copy)
+        return copy
+
+    ref = codes.at[y, x, z, :, A0:B1]
+    g1 = [go(remote(ref, ref, ag, k - 1, on_z(k))) for k in near_z]
+    ref = codes.at[y, x, z, :, C0:WIDE]
+    g1c = [go(remote(ref, ref, ag, 6 + k, on_x(k))) for k in near]
+
+    d0 = pltpu.make_async_copy(trace_ref, traces.at[0:ROWS], local)
+    d0.start()
     d1 = remote(trace_ref, traces.at[ROWS : 2 * ROWS], dd, 0, other)
     d2 = remote(tid_ref, tids.at[1], dd, 1, other)
     d1.start()
     d2.start()
-    traces[0:ROWS] = trace_ref[...]
     tids[0] = tid_ref[...]
 
-    g2 = []
+    def gather_a(i, k):
+        ref = codes.at[y, (x - i) % NX, :, :, A0:A1]
+        return remote(ref, ref, g3a, i * 3 + k - 1, on_y(k))
+
+    def gather_b(j, k):
+        ref = codes.at[(y - j) % NY, x, :, :, B0:B1]
+        return remote(ref, ref, g3b, j * 3 + k - 1, on_x(k))
+
+    def gather_c(j, k):
+        ref = codes.at[(y - j) % NY, :, z, :, C0:WIDE]
+        return remote(ref, ref, g3c, j * 7 + k - 1, on_z(k))
+
     for copy in g1c:
         copy.wait_recv()
-    for k in range(1, NY):
-        ref = codes.at[y, :, z, :, C0:WIDE]
-        g2.append(remote(ref, ref, ag, 9 + k, on_y(k)))
-        g2[-1].start()
-    g2c = list(g2)
+    ref = codes.at[y, :, z, :, C0:WIDE]
+    g2c = [go(remote(ref, ref, ag, 9 + k, on_y(k))) for k in near]
+    for k in near_z:
+        go(gather_c(0, k))
     for copy in g1:
         copy.wait_recv()
-    g2ab = []
-    for k in range(1, 4):
-        ref = codes.at[y, x, :, :, A0:A1]
-        g2ab.append(remote(ref, ref, ag, 12 + k, on_x(k)))
-        ref = codes.at[y, x, :, :, B0:B1]
-        g2ab.append(remote(ref, ref, ag, 15 + k, on_y(k)))
-    for copy in g2ab:
-        copy.start()
-
-    g3 = []
-    for copy in g2c:
-        copy.wait_recv()
-    for k in range(1, NZ):
-        ref = codes.at[:, :, z, :, C0:WIDE]
-        g3.append(remote(ref, ref, ag, 18 + k, on_z(k)))
-        g3[-1].start()
-    for copy in g2ab:
-        copy.wait_recv()
-    for k in range(1, 4):
-        ref = codes.at[y, :, :, :, A0:A1]
-        g3.append(remote(ref, ref, ag, 25 + k, on_y(k)))
-        g3[-1].start()
-        ref = codes.at[:, x, :, :, B0:B1]
-        g3.append(remote(ref, ref, ag, 28 + k, on_x(k)))
-        g3[-1].start()
+    ref_a = codes.at[y, x, :, :, A0:A1]
+    ref_b = codes.at[y, x, :, :, B0:B1]
+    g2a = [go(remote(ref_a, ref_a, ag, 12 + k, on_x(k))) for k in near]
+    g2b = [go(remote(ref_b, ref_b, ag, 15 + k, on_y(k))) for k in near]
+    for k in near:
+        go(gather_a(0, k))
+        go(gather_b(0, k))
+    for n, i in enumerate(near):
+        g2c[n].wait_recv()
+        for k in near_z:
+            go(gather_c(i, k))
+    for n, i in enumerate(near):
+        g2a[n].wait_recv()
+        for k in near:
+            go(gather_a(i, k))
+        g2b[n].wait_recv()
+        for k in near:
+            go(gather_b(i, k))
+    d0.wait()
     d1.wait()
     d2.wait()
-    for copy in g3:
-        copy.wait_recv()
 
     scale = jnp.exp(scale_ref[...])
     shift = shift_ref[...]
@@ -146,7 +156,7 @@
 
     def send_a1(j, q):
         return remote(
-            parts.at[q, :, :, :, A0:A1], recv_a1.at[j - 1], rs, j - 1, on_y(j)
+            parts.at[q, :, :, :, A0:A1], recv_a1.at[j - 1], rs, j - 1, on_y(-j)
         )
 
     def send_b1(j, q, k):
@@ -156,8 +166,18 @@
 
     @pl.loop(0, NY)
     def _(step):
-        j = (step + 1) % NY
-        q = (y + j) % NY
+        j = step + (step // 2) * (5 - 2 * step)
+        q = (y - j) % NY
+
+        @pl.when(j != 0)
+        def _():
+            for i in range(NX):
+                gather_a(i, j).wait_recv()
+
+        for k in range(1, NX):
+            gather_b(j, k).wait_recv()
+        for k in range(1, NZ):
+            gather_c(j, k).wait_recv()
         at = pl.multiple_of(q * SPAN, SPAN)
         for i in range(NX):
             block = codes[q, i, :, :, 0:WIDTH].astype(F32).reshape(NZ * SHARD, WIDTH)
@@ -215,7 +235,7 @@
 
     for k in range(1, NX):
         for j in range(NY):
-            send_b1(j, (y + j) % NY, k).wait_recv()
+            send_b1(j, (y - j) % NY, k).wait_recv()
     for i in range(NY):
         total = parts[i, x, :, :, B0:B1].astype(F32)
         for k in range(NX - 1):
@@ -227,7 +247,7 @@
         b2[-1].start()
 
     for j in range(1, NY):
-        send_a1(j, (y + j) % NY).wait_recv()
+        send_a1(j, (y - j) % NY).wait_recv()
     for i in range(NX):
         total = parts[y, i, :, :, A0:A1].astype(F32)
         for k in range(NY - 1):
@@ -281,13 +301,13 @@
         total = total + recv_ab3[k].astype(F32)
     code_out[:, A0:B1] = total.astype(BF16)
 
-    for copy in g1 + g1c + g2c + g2ab + g3 + c1 + c2 + b2 + a2 + c3 + ab3:
+    for copy in sent + c1 + c2 + b2 + a2 + c3 + ab3:
         copy.wait_send()
     for j in range(NY):
         if j:
-            send_a1(j, (y + j) % NY).wait_send()
+            send_a1(j, (y - j) % NY).wait_send()
         for k in range(1, NX):
-            send_b1(j, (y + j) % NY, k).wait_send()
+            send_b1(j, (y - j) % NY, k).wait_send()
 
 
 def per_device(trace_emb, code_emb, trace_ids, code_ids, log_scale, bias):
@@ -316,20 +336,24 @@
         pltpu.VMEM((ROWS, WIDTH), F32),
         pltpu.VMEM((ROWS, WIDTH), F32),
         pltpu.VMEM((ROWS, WIDTH), F32),
+        dma,
         dma((3,)),
         dma((3,)),
-        dma((32,)),
-        dma((32,)),
+        dma((19,)),
+        dma((19,)),
+        dma((12,)),
+        dma((12,)),
+        dma((12,)),
+        dma((12,)),
+        dma((28,)),
+        dma((28,)),
         dma((41,)),
         dma((41,)),
     ]
     return pl.pallas_call(
         kernel,
-        out_shape=(
-            jax.ShapeDtypeStruct((ROWS, WIDTH), BF16),
-            jax.ShapeDtypeStruct((SHARD, WIDTH), BF16),
-        ),
-        in_specs=[vmem] * 6,
+        out_shape=(pltpu.VMEM((ROWS, WIDTH), BF16), pltpu.VMEM((SHARD, WIDTH), BF16)),
+        in_specs=[pl.BlockSpec(memory_space=pl.ANY)] + [vmem] * 5,
         out_specs=(vmem, vmem),
         scratch_shapes=scratch,
         compiler_params=pltpu.CompilerParams(
@@ -340,7 +364,7 @@
         trace_emb,
         code_emb,
         trace_ids.reshape(1, ROWS),
-        code_ids.reshape(SHARD, 1),
+        code_ids.reshape(1, SHARD),
         log_scale.reshape(1, 1),
         bias.reshape(1, 1),
     )

time: 69.4 us -> 63.2 us (0.911)
  Pallas kernels: 62.5 us -> 59.5 us
  local copies, waits for them, and re-layouts: 4.31 us -> 1.62 us
    pallas_call x1, Pallas kernels: 62.5 us -> 59.5 us  [per_device(): pl.pallas_call(kernel, out_shape=(pltpu.VMEM((ROWS, WIDTH), BF16), pltpu....]
    unnamed x4 -> x2, local copies, waits for them, and re-layouts: 2.99 us -> 1.62 us
    reshape x1 -> x0, local copies, waits for them, and re-layouts: 1.32 us -> none  [per_device(): code_ids.reshape(SHARD, 1)]
where the time goes in v2:
time: 63.2 us; the launch traced here: 63 us
  Pallas kernels  59.5 us (94%)
  between operations  1.93 us (3%)
  local copies, waits for them, and re-layouts  1.62 us (3%)
    pallas_call x1, Pallas kernels, per_device(): pl.pallas_call(kernel, out_shape=(pltpu.VMEM((ROWS, WIDTH), BF16), pltpu....  59.5 us
    unnamed x2, local copies, waits for them, and re-layouts  1.62 us

profile of v2, /device:TPU:16, one launch (start us, length us, event | category | flops | bytes accessed | tf_op | source)
XLA Modules:
  0.0 63.0 jit_solution(15773224823659719037)
XLA Ops:
  1.9 59.5 %contrast.1 = (bf16[512,1152]{1,0:T(8,128)(2,1)S(1)}, bf16[8,1152]{1,0:T(8,128)(2,1)S(1)}) custom-call(bf16[512,1152]{1,0:T(8,128)(2,1)} %trace_ref.1, bf16[8,1152]{1,0:T(8,128)(2,1)} %code_ref.1, s32[1,512]{1,0:T(1,128)} %bitcast.6, s32[1,8]{1,0:T(1,128)} %bitcast.7, f32[1,1]{1,0:T(1,128)} %bitcast.4.scale_ref, f32[1,1]{1,0:T(1,128)} %bitcast.5.shift_ref), custom_call_target="tpu_custom_call" | custom-call | tf_op jit(solution)/shard_map/contrast/pallas_call | solution.py:353
  61.4 1.0 %copy.10 = bf16[512,1152]{1,0:T(8,128)(2,1)} copy(bf16[512,1152]{1,0:T(8,128)(2,1)S(1)} %get-tuple-element.2) | data formatting | bytes 2359296
  62.4 0.6 copy.11

commit v3 on v2

v3 whole, which is shorter than its diff:
```python
import jax
import jax.numpy as jnp
from jax import lax
from jax.experimental import pallas as pl
from jax.experimental.pallas import tpu as pltpu
from jax.sharding import PartitionSpec as P

MESH = pl.DeviceIdType.MESH
F32 = jnp.float32
BF16 = jnp.bfloat16

NY, NX, NZ = 4, 4, 8
SHARD = 8
WIDTH = 1152
ROWS = 512
A0, A1 = 0, 384
B0, B1 = 384, 768
C0, C1 = 768, 1152
GA = slice(0, 384)
GB = slice(384, 768)
GAB = slice(0, 768)
GM = slice(768, 896)
GABM = slice(0, 896)
GC = slice(896, 1280)
WIDE = 1280
SPAN = NX * NZ * SHARD
PLANE = NY * SPAN


def place():
    blk = lax.axis_index("blk")
    group = lax.axis_index("group")
    x = (group // 16) * 2 + blk // 4
    return blk % 4, x, (group // 2) % NZ, group % 2


def device(y, x, z, core):
    return ((x % 2) * 4 + y, ((x // 2) * NZ + z) * 2 + core)


def remote(src, dst, sems, index, target):
    return pltpu.make_async_remote_copy(
        src_ref=src,
        dst_ref=dst,
        send_sem=sems[0].at[index],
        recv_sem=sems[1].at[index],
        device_id=target,
        device_id_type=MESH,
    )


def kernel(
    trace_ref, code_ref, tid_ref, cid_ref, scale_ref, shift_ref,
    trace_out, code_out,
    traces, tids, codes, marks, flat, slopes, parts,
    recv_a1, recv_b1, recv_c1, sum_z, sum_a, sum_b, sum_c, recv_a2, recv_b2, recv_c2,
    sum_ab, recv_ab3, tg_own, tg_send, tg_recv,
    local, s_d, r_d, s_ag, r_ag, s_g3a, r_g3a, s_g3b, r_g3b, s_g3c, r_g3c, s_g1p, r_g1p, s_rs, r_rs, s_rsc, r_rsc, s_rsp, r_rsp,
):
    y, x, z, core = place()
    ag = (s_ag, r_ag)
    rs = (s_rs, r_rs)
    dd = (s_d, r_d)
    g3a, g3b, g3c = (s_g3a, r_g3a), (s_g3b, r_g3b), (s_g3c, r_g3c)
    g1p, rsc, rsp = (s_g1p, r_g1p), (s_rsc, r_rsc), (s_rsp, r_rsp)

    def on_y(k):
        return device((y + k) % NY, x, z, core)

    def on_x(k):
        return device(y, (x + k) % NX, z, core)

    def on_z(k):
        return device(y, x, (z + k) % NZ, core)

    def on_plane(j, i):
        return device((y + j) % NY, (x + i) % NX, z, core)

    other = device(y, x, z, 1 - core)

    barrier = pltpu.get_barrier_semaphore()
    in_plane = [(j, i) for j in (0, 1, 3, 2) for i in (0, 1, 3, 2) if (j, i) != (0, 0)]
    partners = [on_plane(j, i) for j, i in in_plane]
    partners += [on_z(k) for k in range(1, NZ)] + [other]
    for partner in partners:
        pl.semaphore_signal(barrier, inc=1, device_id=partner, device_id_type=MESH)

    spread = jnp.broadcast_to(cid_ref[...], (SHARD, SHARD))
    row = lax.broadcasted_iota(jnp.int32, (SHARD, SHARD), 0)
    column = lax.broadcasted_iota(jnp.int32, (SHARD, SHARD), 1)
    ids = jnp.sum(jnp.where(row == column, spread, 0), axis=1, keepdims=True)
    high = (ids // 16).astype(F32)
    low = (ids % 16).astype(F32)
    lane = lax.broadcasted_iota(jnp.int32, (SHARD, 128), 1)
    tile = jnp.where(lane == 2 * z, high, jnp.where(lane == 2 * z + 1, low, 0.0)).astype(BF16)
    codes[y, x, z, :, GAB] = code_ref[:, 0:768]
    codes[y, x, z, :, GM] = tile
    codes[y, x, z, :, GC] = code_ref[:, 768:WIDTH]
    pl.semaphore_wait(barrier, len(partners))

    near_z = (1, 7, 2, 6, 3, 5, 4)
    near = (1, 3, 2)
    sent = []

    def go(copy):
        copy.start()
        sent.append(copy)
        return copy

    ref = codes.at[y, x, z, :, GABM]
    g1 = [go(remote(ref, ref, ag, k - 1, on_z(k))) for k in near_z]
    ref = codes.at[y, x, z, :, GC]
    g1c = {(j, i): go(remote(ref, ref, g1p, j * 4 + i, on_plane(j, i))) for j, i in in_plane}

    d0 = pltpu.make_async_copy(trace_ref, traces.at[0:ROWS], local)
    d0.start()
    d1 = remote(trace_ref, traces.at[ROWS : 2 * ROWS], dd, 0, other)
    d2 = remote(tid_ref, tids.at[1], dd, 1, other)
    d1.start()
    d2.start()
    tids[0] = tid_ref[...]

    def gather_a(i, way, hop):
        step = 1 - 2 * way
        ref = codes.at[(y - step * (hop - 1)) % NY, (x - i) % NX, :, :, GA]
        return remote(ref, ref, g3a, (way * 4 + i) * 2 + hop - 1, on_y(step))

    def gather_b(j, way, hop):
        step = 1 - 2 * way
        ref = codes.at[(y - j) % NY, (x - step * (hop - 1)) % NX, :, :, GB]
        return remote(ref, ref, g3b, (way * 4 + j) * 2 + hop - 1, on_x(step))

    def gather_c(j, kind):
        half = 2 - 4 * (j // 2)
        start, step = ((0, 1), (0, -1), (0, 2), (0, -2), (-2, 1), (2, -1), (-half, half))[kind]
        ref = codes.at[(y - j) % NY, :, (z + start) % NZ, :, GC]
        return remote(ref, ref, g3c, j * 7 + kind, on_z(step))

    def pass_on(gather, n, way):
        gather(n, way, 1).wait_recv()
        go(gather(n, way, 2))

    def set_out(gather, n):
        for way in (0, 1):
            go(gather(n, way, 1))

    def set_out_c(j):
        for i in near if j == 0 else (0, 1, 3, 2):
            g1c[j, i].wait_recv()
        for kind in (2, 3, 0, 1):
            go(gather_c(j, kind))

    def pass_on_c(j):
        gather_c(j, 2).wait_recv()
        go(gather_c(j, 4))
        if j < 2:
            go(gather_c(j, 6))
        gather_c(j, 3).wait_recv()
        go(gather_c(j, 5))
        if j >= 2:
            go(gather_c(j, 6))

    for j in (0, 1, 3, 2):
        set_out_c(j)
    for copy in g1:
        copy.wait_recv()
    ref_a = codes.at[y, x, :, :, GA]
    ref_b = codes.at[y, x, :, :, GB]
    g2a = [go(remote(ref_a, ref_a, ag, 12 + k, on_x(k))) for k in near]
    g2b = [go(remote(ref_b, ref_b, ag, 15 + k, on_y(k))) for k in near]
    set_out(gather_a, 0)
    set_out(gather_b, 0)
    marks[y, x] = jnp.sum(codes[y, x, :, :, GM].astype(F32), axis=0).astype(BF16)
    ref = marks.at[y, x]
    m2 = [go(remote(ref, ref, ag, 18 + k, on_x(k))) for k in near]
    pass_on_c(0)
    for n in (0, 1):
        g2a[n].wait_recv()
        set_out(gather_a, near[n])
        g2b[n].wait_recv()
        set_out(gather_b, near[n])
    pass_on(gather_a, 0, 0)
    pass_on(gather_b, 0, 0)
    g2a[2].wait_recv()
    set_out(gather_a, 2)
    g2b[2].wait_recv()
    set_out(gather_b, 2)
    pass_on_c(1)
    for copy in m2:
        copy.wait_recv()
    ref = marks.at[y]
    m3 = [go(remote(ref, ref, ag, 21 + k, on_y(k))) for k in near]
    pass_on_c(3)
    pass_on(gather_a, 3, 1)
    pass_on(gather_b, 3, 1)
    pass_on(gather_a, 1, 0)
    pass_on(gather_b, 1, 0)
    pass_on_c(2)
    pass_on(gather_a, 2, 1)
    pass_on(gather_b, 2, 1)
    for copy in m3:
        copy.wait_recv()
    d0.wait()
    d1.wait()
    d2.wait()

    scale = jnp.exp(scale_ref[...])
    shift = shift_ref[...]
    trace_ids = jnp.concatenate([tids[0], tids[1]], axis=1).astype(F32)

    lane = lax.broadcasted_iota(jnp.int32, (1, NZ, 1, 128), 3)
    owner = lax.broadcasted_iota(jnp.int32, (1, NZ, 1, 128), 1)
    pick = jnp.where(lane == 2 * owner, 16.0, jnp.where(lane == 2 * owner + 1, 1.0, 0.0))

    def send_a1(j, q):
        return remote(
            parts.at[q, :, :, :, A0:A1], recv_a1.at[j - 1], rs, j - 1, on_y(-j)
        )

    def send_b1(j, q, k):
        return remote(
            parts.at[q, (x + k) % NX, :, :, B0:B1], recv_b1.at[k - 1, q], rs, 3 + j * 3 + k - 1, on_x(k)
        )

    def send_c1(j, kind):
        q = (y - j) % NY
        half = 2 - 4 * (j // 2)
        if kind in (2, 3):
            source = sum_z.at[kind - 2, q]
        else:
            away = (1, -1, None, None, 3, -3, 4)[kind]
            source = parts.at[q, :, (z + away) % NZ, :, C0:C1]
        step = (1, -1, 2, -2, 1, -1, half)[kind]
        return remote(source, recv_c1.at[kind, q], rsc, j * 7 + kind, on_z(step))

    def relay_c(j):
        q = (y - j) % NY
        for kind in (4, 5, 6):
            send_c1(j, kind).wait_recv()
        upper = jnp.where(j < 2, 1.0, 0.0)
        middle = recv_c1[6, q].astype(F32)
        total = parts[q, :, (z + 2) % NZ, :, C0:C1].astype(F32) + recv_c1[4, q].astype(F32) + upper * middle
        sum_z[0, q] = total.astype(BF16)
        total = parts[q, :, (z + 6) % NZ, :, C0:C1].astype(F32) + recv_c1[5, q].astype(F32) + (1.0 - upper) * middle
        sum_z[1, q] = total.astype(BF16)
        send_c1(j, 2).start()
        send_c1(j, 3).start()

    def block_at(step):
        return step + (step // 2) * (5 - 2 * step)

    @pl.loop(0, NY)
    def _(step):
        j = block_at(step)
        q = (y - j) % NY

        @pl.when(j == 1)
        def _():
            gather_a(2, 0, 1).wait_recv()
            gather_a(3, 0, 1).wait_recv()

        @pl.when(j == 3)
        def _():
            gather_a(0, 1, 1).wait_recv()
            gather_a(1, 1, 1).wait_recv()

        @pl.when(j == 2)
        def _():
            for i in range(NX):
                gather_a(i, i // 2, 2).wait_recv()

        gather_b(j, 1 - j // 2, 1).wait_recv()
        gather_b(j, j // 2, 2).wait_recv()
        for kind in (0, 1, 4, 5, 6):
            gather_c(j, kind).wait_recv()
        at = pl.multiple_of(q * SPAN, SPAN)
        for i in range(NX):
            rows = pl.ds(at + i * NZ * SHARD, NZ * SHARD)
            block = codes[q, i, :, :, GAB].astype(F32).reshape(NZ * SHARD, 768)
            flat[rows, 0:768] = block.astype(BF16)
            block = codes[q, i, :, :, GC].astype(F32).reshape(NZ * SHARD, 384)
            flat[rows, 768:WIDTH] = block.astype(BF16)
        spread = marks[q].astype(F32).reshape(NX, 1, SHARD, 128)
        code_ids = jnp.sum(spread * pick, axis=3, keepdims=True).reshape(SPAN, 1)
        logits = lax.dot_general(
            flat[pl.ds(at, SPAN), :], traces[...], (((1,), (1,)), ((), ())), preferred_element_type=F32
        )
        logits = logits * scale + shift
        same = code_ids == trace_ids
        raised = jnp.exp(jnp.where(same, logits, -logits))
        slope = jnp.where(same, -scale, scale) / (1.0 + raised)
        slopes[pl.ds(at, SPAN), :] = slope.astype(BF16)
        grad = jnp.dot(slopes[pl.ds(at, SPAN), :], traces[...], preferred_element_type=F32)
        parts[q] = grad.reshape(NX, NZ, SHARD, WIDTH).astype(BF16)

        @pl.when(j != 0)
        def _():
            send_a1(j, q).start()

        for kind in (4, 5, 6):
            send_c1(j, kind).start()
        for k in range(1, NX):
            send_b1(j, q, k).start()
        for kind in (0, 1):
            send_c1(j, kind).start()

        @pl.when(step >= 2)
        def _():
            relay_c(block_at(step - 2))

    relay_c(3)

    def trace_rows(first):
        return lax.dot_general(
            slopes[:, first : first + 256], flat[...], (((0,), (0,)), ((), ())), preferred_element_type=F32
        )

    for n in range(2):
        tg_send[n * 256 : n * 256 + 256, :] = trace_rows(ROWS + n * 256)
    d3 = remote(tg_send, tg_recv, dd, 2, other)
    d3.start()
    relay_c(2)
    for n in range(2):
        tg_own[n * 256 : n * 256 + 256, :] = trace_rows(n * 256)

    for k in range(1, NX):
        for j in range(NY):
            send_b1(j, (y - j) % NY, k).wait_recv()
    for i in range(NY):
        total = parts[i, x, :, :, B0:B1].astype(F32)
        for k in range(NX - 1):
            total = total + recv_b1[k, i].astype(F32)
        sum_b[i] = total.astype(BF16)
    b2 = []
    for k in range(1, NY):
        b2.append(remote(sum_b.at[(y + k) % NY], recv_b2.at[k - 1], rs, 24 + k, on_y(k)))
        b2[-1].start()

    for j in range(1, NY):
        send_a1(j, (y - j) % NY).wait_recv()
    for i in range(NX):
        total = parts[y, i, :, :, A0:A1].astype(F32)
        for k in range(NY - 1):
            total = total + recv_a1[k, i].astype(F32)
        sum_a[i] = total.astype(BF16)
    a2 = []
    for k in range(1, NX):
        a2.append(remote(sum_a.at[(x + k) % NX], recv_a2.at[k - 1], rs, 27 + k, on_x(k)))
        a2[-1].start()

    for j in range(NY):
        for kind in range(4):
            send_c1(j, kind).wait_recv()
    for i in range(NY):
        total = parts[i, :, z, :, C0:C1].astype(F32)
        for kind in range(4):
            total = total + recv_c1[kind, i].astype(F32)
        sum_c[i] = total.astype(BF16)
    c2 = []
    for j, i in in_plane:
        c2.append(
            remote(sum_c.at[(y + j) % NY, (x + i) % NX], recv_c2.at[j * 4 + i], rsp, j * 4 + i, on_plane(j, i))
        )
        c2[-1].start()
    for copy in b2:
        copy.wait_recv()
    total = sum_b[y].astype(F32)
    for k in range(NY - 1):
        total = total + recv_b2[k].astype(F32)
    sum_ab[:, :, B0:B1] = total.astype(BF16)
    for copy in a2:
        copy.wait_recv()
    total = sum_a[x].astype(F32)
    for k in range(NX - 1):
        total = total + recv_a2[k].astype(F32)
    sum_ab[:, :, A0:A1] = total.astype(BF16)
    ab3 = []
    for k in range(1, NZ):
        ab3.append(remote(sum_ab.at[(z + k) % NZ], recv_ab3.at[k - 1], rs, 33 + k, on_z(k)))
        ab3[-1].start()

    d3.wait()
    trace_out[...] = (tg_own[...] + tg_recv[...]).astype(BF16)

    for copy in c2:
        copy.wait_recv()
    total = sum_c[y, x].astype(F32)
    for j, i in in_plane:
        total = total + recv_c2[j * 4 + i].astype(F32)
    code_out[:, C0:C1] = total.astype(BF16)
    for copy in ab3:
        copy.wait_recv()
    total = sum_ab[z].astype(F32)
    for k in range(NZ - 1):
        total = total + recv_ab3[k].astype(F32)
    code_out[:, A0:B1] = total.astype(BF16)

    for copy in sent + c2 + b2 + a2 + ab3:
        copy.wait_send()
    for j in range(NY):
        if j:
            send_a1(j, (y - j) % NY).wait_send()
        for k in range(1, NX):
            send_b1(j, (y - j) % NY, k).wait_send()
        for kind in range(7):
            send_c1(j, kind).wait_send()


def per_device(trace_emb, code_emb, trace_ids, code_ids, log_scale, bias):
    vmem = pl.BlockSpec(memory_space=pltpu.VMEM)
    dma = pltpu.SemaphoreType.DMA
    scratch = [
        pltpu.VMEM((2 * ROWS, WIDTH), BF16),
        pltpu.VMEM((2, 1, ROWS), jnp.int32),
        pltpu.VMEM((NY, NX, NZ, SHARD, WIDE), BF16),
        pltpu.VMEM((NY, NX, SHARD, 128), BF16),
        pltpu.VMEM((PLANE, WIDTH), BF16),
        pltpu.VMEM((PLANE, 2 * ROWS), BF16),
        pltpu.VMEM((NY, NX, NZ, SHARD, WIDTH), BF16),
        pltpu.VMEM((NY - 1, NX, NZ, SHARD, A1 - A0), BF16),
        pltpu.VMEM((NX - 1, NY, NZ, SHARD, B1 - B0), BF16),
        pltpu.VMEM((7, NY, NX, SHARD, C1 - C0), BF16),
        pltpu.VMEM((2, NY, NX, SHARD, C1 - C0), BF16),
        pltpu.VMEM((NX, NZ, SHARD, A1 - A0), BF16),
        pltpu.VMEM((NY, NZ, SHARD, B1 - B0), BF16),
        pltpu.VMEM((NY, NX, SHARD, C1 - C0), BF16),
        pltpu.VMEM((NX - 1, NZ, SHARD, A1 - A0), BF16),
        pltpu.VMEM((NY - 1, NZ, SHARD, B1 - B0), BF16),
        pltpu.VMEM((NY * NX, SHARD, C1 - C0), BF16),
        pltpu.VMEM((NZ, SHARD, B1 - A0), BF16),
        pltpu.VMEM((NZ - 1, SHARD, B1 - A0), BF16),
        pltpu.VMEM((ROWS, WIDTH), F32),
        pltpu.VMEM((ROWS, WIDTH), F32),
        pltpu.VMEM((ROWS, WIDTH), F32),
        dma,
        dma((3,)),
        dma((3,)),
        dma((25,)),
        dma((25,)),
        dma((16,)),
        dma((16,)),
        dma((16,)),
        dma((16,)),
        dma((28,)),
        dma((28,)),
        dma((16,)),
        dma((16,)),
        dma((41,)),
        dma((41,)),
        dma((28,)),
        dma((28,)),
        dma((16,)),
        dma((16,)),
    ]
    return pl.pallas_call(
        kernel,
        out_shape=(pltpu.VMEM((ROWS, WIDTH), BF16), pltpu.VMEM((SHARD, WIDTH), BF16)),
        in_specs=[pl.BlockSpec(memory_space=pl.ANY)] + [vmem] * 5,
        out_specs=(vmem, vmem),
        scratch_shapes=scratch,
        compiler_params=pltpu.CompilerParams(
            collective_id=0, has_side_effects=True, vmem_limit_bytes=56 * 2**20
        ),
        name="contrast",
    )(
        trace_emb,
        code_emb,
        trace_ids.reshape(1, ROWS),
        code_ids.reshape(1, SHARD),
        log_scale.reshape(1, 1),
        bias.reshape(1, 1),
    )


def solution(mesh):
    placed = (
        P(("blk", "group"), None),
        P(("blk", "group"), None),
        P(("blk", "group")),
        P(("blk", "group")),
        P(),
        P(),
    )
    return jax.shard_map(
        per_device,
        mesh=mesh,
        in_specs=placed,
        out_specs=(P(("blk", "group"), None), P(("blk", "group"), None)),
        check_vma=False,
    )
```

time: 63.2 us -> 58.3 us (0.922)
  Pallas kernels: 59.5 us -> 54 us
    pallas_call x1, Pallas kernels: 59.5 us -> 54 us  [per_device(): pl.pallas_call(kernel, out_shape=(pltpu.VMEM((ROWS, WIDTH), BF16), pltpu....]
where the time goes in v3:
time: 58.3 us; the launch traced here: 57.6 us
  Pallas kernels  54 us (93%)
  between operations  1.93 us (3%)
  local copies, waits for them, and re-layouts  1.62 us (3%)
    pallas_call x1, Pallas kernels, per_device(): pl.pallas_call(kernel, out_shape=(pltpu.VMEM((ROWS, WIDTH), BF16), pltpu....  54 us
    unnamed x2, local copies, waits for them, and re-layouts  1.62 us

profile of v3, /device:TPU:16, one launch (start us, length us, event | category | flops | bytes accessed | tf_op | source)
XLA Modules:
  0.0 57.6 jit_solution(11224163040795971229)
XLA Ops:
  1.9 54.0 %contrast.1 = (bf16[512,1152]{1,0:T(8,128)(2,1)S(1)}, bf16[8,1152]{1,0:T(8,128)(2,1)S(1)}) custom-call(bf16[512,1152]{1,0:T(8,128)(2,1)} %trace_ref.1, bf16[8,1152]{1,0:T(8,128)(2,1)} %code_ref.1, s32[1,512]{1,0:T(1,128)} %bitcast.6, s32[1,8]{1,0:T(1,128)} %bitcast.7, f32[1,1]{1,0:T(1,128)} %bitcast.4.scale_ref, f32[1,1]{1,0:T(1,128)} %bitcast.5.shift_ref), custom_call_target="tpu_custom_call" | custom-call | tf_op jit(solution)/shard_map/contrast/pallas_call | solution.py:455
  55.9 1.0 %copy.10 = bf16[512,1152]{1,0:T(8,128)(2,1)} copy(bf16[512,1152]{1,0:T(8,128)(2,1)S(1)} %get-tuple-element.2) | data formatting | bytes 2359296
  57.0 0.6 %copy.11 = bf16[8,1152]{1,0:T(8,128)(2,1)} copy(bf16[8,1152]{1,0:T(8,128)(2,1)S(1)} %get-tuple-element.3) | data formatting | bytes 36864

commit v4 on v3

--- a/solution.py
+++ b/solution.py
@@ -52,7 +52,7 @@
 def kernel(
     trace_ref, code_ref, tid_ref, cid_ref, scale_ref, shift_ref,
     trace_out, code_out,
-    traces, tids, codes, marks, flat, slopes, parts,
+    code_v, cid_v, scale_v, shift_v, traces, tids, codes, marks, flat, slopes, parts,
     recv_a1, recv_b1, recv_c1, sum_z, sum_a, sum_b, sum_c, recv_a2, recv_b2, recv_c2,
     sum_ab, recv_ab3, tg_own, tg_send, tg_recv,
     local, s_d, r_d, s_ag, r_ag, s_g3a, r_g3a, s_g3b, r_g3b, s_g3c, r_g3c, s_g1p, r_g1p, s_rs, r_rs, s_rsc, r_rsc, s_rsp, r_rsp,
@@ -78,6 +78,14 @@
 
     other = device(y, x, z, 1 - core)
 
+    pairs = (
+        (trace_ref, traces.at[0:ROWS]), (code_ref, code_v), (cid_ref, cid_v),
+        (tid_ref, tids.at[0]), (scale_ref, scale_v), (shift_ref, shift_v),
+    )
+    fetch = [pltpu.make_async_copy(src, dst, local.at[n]) for n, (src, dst) in enumerate(pairs)]
+    for n in (1, 2, 0, 3, 4, 5):
+        fetch[n].start()
+
     barrier = pltpu.get_barrier_semaphore()
     in_plane = [(j, i) for j in (0, 1, 3, 2) for i in (0, 1, 3, 2) if (j, i) != (0, 0)]
     partners = [on_plane(j, i) for j, i in in_plane]
@@ -85,7 +93,9 @@
     for partner in partners:
         pl.semaphore_signal(barrier, inc=1, device_id=partner, device_id_type=MESH)
 
-    spread = jnp.broadcast_to(cid_ref[...], (SHARD, SHARD))
+    fetch[1].wait()
+    fetch[2].wait()
+    spread = jnp.broadcast_to(cid_v[...], (SHARD, SHARD))
     row = lax.broadcasted_iota(jnp.int32, (SHARD, SHARD), 0)
     column = lax.broadcasted_iota(jnp.int32, (SHARD, SHARD), 1)
     ids = jnp.sum(jnp.where(row == column, spread, 0), axis=1, keepdims=True)
@@ -93,9 +103,9 @@
     low = (ids % 16).astype(F32)
     lane = lax.broadcasted_iota(jnp.int32, (SHARD, 128), 1)
     tile = jnp.where(lane == 2 * z, high, jnp.where(lane == 2 * z + 1, low, 0.0)).astype(BF16)
-    codes[y, x, z, :, GAB] = code_ref[:, 0:768]
+    codes[y, x, z, :, GAB] = code_v[:, 0:768]
     codes[y, x, z, :, GM] = tile
-    codes[y, x, z, :, GC] = code_ref[:, 768:WIDTH]
+    codes[y, x, z, :, GC] = code_v[:, 768:WIDTH]
     pl.semaphore_wait(barrier, len(partners))
 
     near_z = (1, 7, 2, 6, 3, 5, 4)
@@ -112,13 +122,10 @@
     ref = codes.at[y, x, z, :, GC]
     g1c = {(j, i): go(remote(ref, ref, g1p, j * 4 + i, on_plane(j, i))) for j, i in in_plane}
 
-    d0 = pltpu.make_async_copy(trace_ref, traces.at[0:ROWS], local)
-    d0.start()
     d1 = remote(trace_ref, traces.at[ROWS : 2 * ROWS], dd, 0, other)
     d2 = remote(tid_ref, tids.at[1], dd, 1, other)
     d1.start()
     d2.start()
-    tids[0] = tid_ref[...]
 
     def gather_a(i, way, hop):
         step = 1 - 2 * way
@@ -200,27 +207,41 @@
     pass_on(gather_b, 2, 1)
     for copy in m3:
         copy.wait_recv()
-    d0.wait()
+    for n in (0, 3, 4, 5):
+        fetch[n].wait()
     d1.wait()
     d2.wait()
 
-    scale = jnp.exp(scale_ref[...])
-    shift = shift_ref[...]
+    scale = jnp.exp(scale_v[...])
+    shift = shift_v[...]
     trace_ids = jnp.concatenate([tids[0], tids[1]], axis=1).astype(F32)
 
     lane = lax.broadcasted_iota(jnp.int32, (1, NZ, 1, 128), 3)
     owner = lax.broadcasted_iota(jnp.int32, (1, NZ, 1, 128), 1)
     pick = jnp.where(lane == 2 * owner, 16.0, jnp.where(lane == 2 * owner + 1, 1.0, 0.0))
 
-    def send_a1(j, q):
+    def send_a1(j, i):
+        q = (y - j) % NY
         return remote(
-            parts.at[q, :, :, :, A0:A1], recv_a1.at[j - 1], rs, j - 1, on_y(-j)
+            parts.at[q, (x + i) % NX, :, :, A0:A1], recv_a1.at[j - 1, i], rs, (j - 1) * 4 + i, on_y(-j)
         )
 
-    def send_b1(j, q, k):
+    def send_b1(j, k):
+        q = (y - j) % NY
         return remote(
-            parts.at[q, (x + k) % NX, :, :, B0:B1], recv_b1.at[k - 1, q], rs, 3 + j * 3 + k - 1, on_x(k)
+            parts.at[q, (x + k) % NX, :, :, B0:B1], recv_b1.at[k - 1, j], rs, 12 + j * 3 + k - 1, on_x(k)
         )
+
+    def send_b2(j):
+        return remote(sum_b.at[j], recv_b2.at[j - 1], rs, 23 + j, on_y(-j))
+
+    def relay_b(j):
+        for k in near:
+            send_b1(j, k).wait_recv()
+        total = parts[(y - j) % NY, x, :, :, B0:B1].astype(F32)
+        for k in near:
+            total = total + recv_b1[k - 1, j].astype(F32)
+        sum_b[j] = total.astype(BF16)
 
     def send_c1(j, kind):
         q = (y - j) % NY
@@ -295,19 +316,27 @@
 
         @pl.when(j != 0)
         def _():
-            send_a1(j, q).start()
+            for i in (2, 1, 3, 0):
+                send_a1(j, i).start()
 
         for kind in (4, 5, 6):
             send_c1(j, kind).start()
         for k in range(1, NX):
-            send_b1(j, q, k).start()
+            send_b1(j, k).start()
         for kind in (0, 1):
             send_c1(j, kind).start()
 
         @pl.when(step >= 2)
         def _():
             relay_c(block_at(step - 2))
-
+            relay_b(block_at(step - 2))
+
+            @pl.when(step == 3)
+            def _():
+                send_b2(1).start()
+
+    relay_b(3)
+    send_b2(3).start()
     relay_c(3)
 
     def trace_rows(first):
@@ -319,35 +348,21 @@
         tg_send[n * 256 : n * 256 + 256, :] = trace_rows(ROWS + n * 256)
     d3 = remote(tg_send, tg_recv, dd, 2, other)
     d3.start()
+
+    relay_b(2)
+    send_b2(2).start()
     relay_c(2)
-    for n in range(2):
-        tg_own[n * 256 : n * 256 + 256, :] = trace_rows(n * 256)
-
-    for k in range(1, NX):
-        for j in range(NY):
-            send_b1(j, (y - j) % NY, k).wait_recv()
-    for i in range(NY):
-        total = parts[i, x, :, :, B0:B1].astype(F32)
-        for k in range(NX - 1):
-            total = total + recv_b1[k, i].astype(F32)
-        sum_b[i] = total.astype(BF16)
-    b2 = []
-    for k in range(1, NY):
-        b2.append(remote(sum_b.at[(y + k) % NY], recv_b2.at[k - 1], rs, 24 + k, on_y(k)))
-        b2[-1].start()
-
-    for j in range(1, NY):
-        send_a1(j, (y - j) % NY).wait_recv()
-    for i in range(NX):
-        total = parts[y, i, :, :, A0:A1].astype(F32)
-        for k in range(NY - 1):
-            total = total + recv_a1[k, i].astype(F32)
+    a2 = []
+    for i in (2, 1, 3, 0):
+        for j in near:
+            send_a1(j, i).wait_recv()
+        total = parts[y, (x + i) % NX, :, :, A0:A1].astype(F32)
+        for j in near:
+            total = total + recv_a1[j - 1, i].astype(F32)
         sum_a[i] = total.astype(BF16)
-    a2 = []
-    for k in range(1, NX):
-        a2.append(remote(sum_a.at[(x + k) % NX], recv_a2.at[k - 1], rs, 27 + k, on_x(k)))
-        a2[-1].start()
-
+        if i:
+            a2.append(remote(sum_a.at[i], recv_a2.at[i - 1], rs, 26 + i, on_x(i)))
+            a2[-1].start()
     for j in range(NY):
         for kind in range(4):
             send_c1(j, kind).wait_recv()
@@ -362,23 +377,26 @@
             remote(sum_c.at[(y + j) % NY, (x + i) % NX], recv_c2.at[j * 4 + i], rsp, j * 4 + i, on_plane(j, i))
         )
         c2[-1].start()
-    for copy in b2:
-        copy.wait_recv()
-    total = sum_b[y].astype(F32)
+
+    for j in near:
+        send_b2(j).wait_recv()
+    total = sum_b[0].astype(F32)
     for k in range(NY - 1):
         total = total + recv_b2[k].astype(F32)
     sum_ab[:, :, B0:B1] = total.astype(BF16)
     for copy in a2:
         copy.wait_recv()
-    total = sum_a[x].astype(F32)
+    total = sum_a[0].astype(F32)
     for k in range(NX - 1):
         total = total + recv_a2[k].astype(F32)
     sum_ab[:, :, A0:A1] = total.astype(BF16)
     ab3 = []
-    for k in range(1, NZ):
-        ab3.append(remote(sum_ab.at[(z + k) % NZ], recv_ab3.at[k - 1], rs, 33 + k, on_z(k)))
+    for k in near_z:
+        ab3.append(remote(sum_ab.at[(z + k) % NZ], recv_ab3.at[k - 1], rs, 29 + k, on_z(k)))
         ab3[-1].start()
 
+    for n in range(2):
+        tg_own[n * 256 : n * 256 + 256, :] = trace_rows(n * 256)
     d3.wait()
     trace_out[...] = (tg_own[...] + tg_recv[...]).astype(BF16)
 
@@ -395,13 +413,15 @@
         total = total + recv_ab3[k].astype(F32)
     code_out[:, A0:B1] = total.astype(BF16)
 
-    for copy in sent + c2 + b2 + a2 + ab3:
+    for copy in sent + c2 + a2 + ab3:
         copy.wait_send()
     for j in range(NY):
         if j:
-            send_a1(j, (y - j) % NY).wait_send()
-        for k in range(1, NX):
-            send_b1(j, (y - j) % NY, k).wait_send()
+            send_b2(j).wait_send()
+            for i in range(NX):
+                send_a1(j, i).wait_send()
+        for k in near:
+            send_b1(j, k).wait_send()
         for kind in range(7):
             send_c1(j, kind).wait_send()
 
@@ -410,6 +430,10 @@
     vmem = pl.BlockSpec(memory_space=pltpu.VMEM)
     dma = pltpu.SemaphoreType.DMA
     scratch = [
+        pltpu.VMEM((SHARD, WIDTH), BF16),
+        pltpu.VMEM((1, SHARD), jnp.int32),
+        pltpu.VMEM((1, 1), F32),
+        pltpu.VMEM((1, 1), F32),
         pltpu.VMEM((2 * ROWS, WIDTH), BF16),
         pltpu.VMEM((2, 1, ROWS), jnp.int32),
         pltpu.VMEM((NY, NX, NZ, SHARD, WIDE), BF16),
@@ -432,7 +456,7 @@
         pltpu.VMEM((ROWS, WIDTH), F32),
         pltpu.VMEM((ROWS, WIDTH), F32),
         pltpu.VMEM((ROWS, WIDTH), F32),
-        dma,
+        dma((6,)),
         dma((3,)),
         dma((3,)),
         dma((25,)),
@@ -455,7 +479,7 @@
     return pl.pallas_call(
         kernel,
         out_shape=(pltpu.VMEM((ROWS, WIDTH), BF16), pltpu.VMEM((SHARD, WIDTH), BF16)),
-        in_specs=[pl.BlockSpec(memory_space=pl.ANY)] + [vmem] * 5,
+        in_specs=[pl.BlockSpec(memory_space=pl.ANY)] * 6,
         out_specs=(vmem, vmem),
         scratch_shapes=scratch,
         compiler_params=pltpu.CompilerParams(

time: 58.3 us -> 56.3 us (0.966)
  Pallas kernels: 54 us -> 52.3 us
    pallas_call x1, Pallas kernels: 54 us -> 52.3 us  [per_device(): pl.pallas_call(kernel, out_shape=(pltpu.VMEM((ROWS, WIDTH), BF16), pltpu....]
where the time goes in v4:
time: 56.3 us; the launch traced here: 55.8 us
  Pallas kernels  52.3 us (93%)
  between operations  1.93 us (3%)
  local copies, waits for them, and re-layouts  1.62 us (3%)
    pallas_call x1, Pallas kernels, per_device(): pl.pallas_call(kernel, out_shape=(pltpu.VMEM((ROWS, WIDTH), BF16), pltpu....  52.3 us
    unnamed x2, local copies, waits for them, and re-layouts  1.62 us

profile of v4, /device:TPU:16, one launch (start us, length us, event | category | flops | bytes accessed | tf_op | source)
XLA Modules:
  0.0 55.8 jit_solution(6697959531798708523)
XLA Ops:
  1.9 52.3 %contrast.1 = (bf16[512,1152]{1,0:T(8,128)(2,1)S(1)}, bf16[8,1152]{1,0:T(8,128)(2,1)S(1)}) custom-call(bf16[512,1152]{1,0:T(8,128)(2,1)} %trace_ref.1, bf16[8,1152]{1,0:T(8,128)(2,1)} %code_ref.1, s32[1,512]{1,0:T(1,128)} %bitcast.6, s32[1,8]{1,0:T(1,128)} %bitcast.7, f32[1,1]{1,0:T(1,128)} %bitcast.4.scale_ref, f32[1,1]{1,0:T(1,128)} %bitcast.5.shift_ref), custom_call_target="tpu_custom_call" | custom-call | tf_op jit(solution)/shard_map/contrast/pallas_call | solution.py:479
  54.2 1.0 %copy.10 = bf16[512,1152]{1,0:T(8,128)(2,1)} copy(bf16[512,1152]{1,0:T(8,128)(2,1)S(1)} %get-tuple-element.2) | data formatting | bytes 2359296
  55.2 0.6 %copy.11 = bf16[8,1152]{1,0:T(8,128)(2,1)} copy(bf16[8,1152]{1,0:T(8,128)(2,1)S(1)} %get-tuple-element.3) | data formatting | bytes 36864

commit v5 on v4

--- a/solution.py
+++ b/solution.py
@@ -24,6 +24,9 @@
 GC = slice(896, 1280)
 WIDE = 1280
 SPAN = NX * NZ * SHARD
+UP = (0, 1, 7, 2, 6, 3, 5, 4)
+SLOT = tuple(UP.index(d) for d in range(NZ))
+HALF = NZ // 2
 PLANE = NY * SPAN
 
 
@@ -55,13 +58,14 @@
     code_v, cid_v, scale_v, shift_v, traces, tids, codes, marks, flat, slopes, parts,
     recv_a1, recv_b1, recv_c1, sum_z, sum_a, sum_b, sum_c, recv_a2, recv_b2, recv_c2,
     sum_ab, recv_ab3, tg_own, tg_send, tg_recv,
-    local, s_d, r_d, s_ag, r_ag, s_g3a, r_g3a, s_g3b, r_g3b, s_g3c, r_g3c, s_g1p, r_g1p, s_rs, r_rs, s_rsc, r_rsc, s_rsp, r_rsp,
+    local, s_d, r_d, s_ag, r_ag, s_g3a, r_g3a, s_g3b, r_g3b, s_g3c, r_g3c, s_g1p, r_g1p, s_g2s, r_g2s, s_rs, r_rs, s_rsc, r_rsc, s_rsp, r_rsp,
 ):
     y, x, z, core = place()
     ag = (s_ag, r_ag)
     rs = (s_rs, r_rs)
     dd = (s_d, r_d)
     g3a, g3b, g3c = (s_g3a, r_g3a), (s_g3b, r_g3b), (s_g3c, r_g3c)
+    g2s = (s_g2s, r_g2s)
     g1p, rsc, rsp = (s_g1p, r_g1p), (s_rsc, r_rsc), (s_rsp, r_rsp)
 
     def on_y(k):
@@ -103,9 +107,9 @@
     low = (ids % 16).astype(F32)
     lane = lax.broadcasted_iota(jnp.int32, (SHARD, 128), 1)
     tile = jnp.where(lane == 2 * z, high, jnp.where(lane == 2 * z + 1, low, 0.0)).astype(BF16)
-    codes[y, x, z, :, GAB] = code_v[:, 0:768]
-    codes[y, x, z, :, GM] = tile
-    codes[y, x, z, :, GC] = code_v[:, 768:WIDTH]
+    codes[y, x, 0, :, GAB] = code_v[:, 0:768]
+    codes[y, x, 0, :, GM] = tile
+    codes[y, x, 0, :, GC] = code_v[:, 768:WIDTH]
     pl.semaphore_wait(barrier, len(partners))
 
     near_z = (1, 7, 2, 6, 3, 5, 4)
@@ -117,9 +121,11 @@
         sent.append(copy)
         return copy
 
-    ref = codes.at[y, x, z, :, GABM]
-    g1 = [go(remote(ref, ref, ag, k - 1, on_z(k))) for k in near_z]
-    ref = codes.at[y, x, z, :, GC]
+    g1 = {}
+    for k in (1, 7, 6, 2, 5, 3, 4):
+        source, target = codes.at[y, x, 0, :, GABM], codes.at[y, x, SLOT[NZ - k], :, GABM]
+        g1[k] = go(remote(source, target, ag, k - 1, on_z(k)))
+    ref = codes.at[y, x, 0, :, GC]
     g1c = {(j, i): go(remote(ref, ref, g1p, j * 4 + i, on_plane(j, i))) for j, i in in_plane}
 
     d1 = remote(trace_ref, traces.at[ROWS : 2 * ROWS], dd, 0, other)
@@ -127,29 +133,52 @@
     d1.start()
     d2.start()
 
-    def gather_a(i, way, hop):
+    def gather_a(i, way, hop, half):
         step = 1 - 2 * way
-        ref = codes.at[(y - step * (hop - 1)) % NY, (x - i) % NX, :, :, GA]
-        return remote(ref, ref, g3a, (way * 4 + i) * 2 + hop - 1, on_y(step))
-
-    def gather_b(j, way, hop):
+        ref = codes.at[(y - step * (hop - 1)) % NY, (x - i) % NX, pl.ds(half * HALF, HALF), :, GA]
+        return remote(ref, ref, g3a, ((half * 2 + way) * 4 + i) * 2 + hop - 1, on_y(step))
+
+    def gather_b(j, way, hop, half):
         step = 1 - 2 * way
-        ref = codes.at[(y - j) % NY, (x - step * (hop - 1)) % NX, :, :, GB]
-        return remote(ref, ref, g3b, (way * 4 + j) * 2 + hop - 1, on_x(step))
+        ref = codes.at[(y - j) % NY, (x - step * (hop - 1)) % NX, pl.ds(half * HALF, HALF), :, GB]
+        return remote(ref, ref, g3b, ((half * 2 + way) * 4 + j) * 2 + hop - 1, on_x(step))
 
     def gather_c(j, kind):
-        half = 2 - 4 * (j // 2)
-        start, step = ((0, 1), (0, -1), (0, 2), (0, -2), (-2, 1), (2, -1), (-half, half))[kind]
-        ref = codes.at[(y - j) % NY, :, (z + start) % NZ, :, GC]
-        return remote(ref, ref, g3c, j * 7 + kind, on_z(step))
-
-    def pass_on(gather, n, way):
-        gather(n, way, 1).wait_recv()
-        go(gather(n, way, 2))
-
-    def set_out(gather, n):
+        start, step = ((0, 1), (0, -1), (0, 2), (0, -2), (-2, 1), (2, -1), (None, 2 - 4 * (j // 2)))[kind]
+        if kind == 6:
+            here, there = SLOT[6] + (j // 2) * (SLOT[2] - SLOT[6]), SLOT[4]
+        else:
+            here, there = SLOT[start % NZ], SLOT[(start - step) % NZ]
+        row = (y - j) % NY
+        return remote(codes.at[row, :, here, :, GC], codes.at[row, :, there, :, GC], g3c, j * 7 + kind, on_z(step))
+
+    def pass_on(n, half):
+        for gather in (gather_a, gather_b):
+            gather(n, n // 2, 1, half).wait_recv()
+            go(gather(n, n // 2, 2, half))
+
+    def set_out(gather, n, half):
         for way in (0, 1):
-            go(gather(n, way, 1))
+            go(gather(n, way, 1, half))
+
+    def set_out_both(n, half):
+        if n:
+            g2a[half, n].wait_recv()
+        set_out(gather_a, n, half)
+        if n:
+            g2b[half, n].wait_recv()
+        set_out(gather_b, n, half)
+
+    g2a, g2b = {}, {}
+
+    def spread_both(half):
+        part = pl.ds(half * HALF, HALF)
+        for k in near:
+            ref = codes.at[y, x, part, :, GA]
+            g2a[half, k] = go(remote(ref, ref, g2s, half * 6 + k - 1, on_x(k)))
+            ref = codes.at[y, x, part, :, GB]
+            g2b[half, k] = go(remote(ref, ref, g2s, half * 6 + 2 + k, on_y(k)))
+        set_out_both(0, half)
 
     def set_out_c(j):
         for i in near if j == 0 else (0, 1, 3, 2):
@@ -167,44 +196,41 @@
         if j >= 2:
             go(gather_c(j, 6))
 
-    for j in (0, 1, 3, 2):
-        set_out_c(j)
-    for copy in g1:
-        copy.wait_recv()
-    ref_a = codes.at[y, x, :, :, GA]
-    ref_b = codes.at[y, x, :, :, GB]
-    g2a = [go(remote(ref_a, ref_a, ag, 12 + k, on_x(k))) for k in near]
-    g2b = [go(remote(ref_b, ref_b, ag, 15 + k, on_y(k))) for k in near]
-    set_out(gather_a, 0)
-    set_out(gather_b, 0)
+    set_out_c(0)
+    for k in (1, 7, 6):
+        g1[k].wait_recv()
+    spread_both(0)
+    set_out_c(1)
+    set_out_c(3)
+    for k in (2, 5, 3, 4):
+        g1[k].wait_recv()
+    spread_both(1)
+    set_out_c(2)
     marks[y, x] = jnp.sum(codes[y, x, :, :, GM].astype(F32), axis=0).astype(BF16)
     ref = marks.at[y, x]
     m2 = [go(remote(ref, ref, ag, 18 + k, on_x(k))) for k in near]
+    set_out_both(1, 0)
+    set_out_both(3, 0)
     pass_on_c(0)
-    for n in (0, 1):
-        g2a[n].wait_recv()
-        set_out(gather_a, near[n])
-        g2b[n].wait_recv()
-        set_out(gather_b, near[n])
-    pass_on(gather_a, 0, 0)
-    pass_on(gather_b, 0, 0)
-    g2a[2].wait_recv()
-    set_out(gather_a, 2)
-    g2b[2].wait_recv()
-    set_out(gather_b, 2)
+    pass_on(0, 0)
+    set_out_both(2, 0)
+    set_out_both(1, 1)
+    set_out_both(3, 1)
+    pass_on(0, 1)
+    set_out_both(2, 1)
     pass_on_c(1)
     for copy in m2:
         copy.wait_recv()
     ref = marks.at[y]
     m3 = [go(remote(ref, ref, ag, 21 + k, on_y(k))) for k in near]
+    pass_on(3, 0)
+    pass_on(1, 0)
     pass_on_c(3)
-    pass_on(gather_a, 3, 1)
-    pass_on(gather_b, 3, 1)
-    pass_on(gather_a, 1, 0)
-    pass_on(gather_b, 1, 0)
+    pass_on(2, 0)
+    pass_on(3, 1)
+    pass_on(1, 1)
     pass_on_c(2)
-    pass_on(gather_a, 2, 1)
-    pass_on(gather_b, 2, 1)
+    pass_on(2, 1)
     for copy in m3:
         copy.wait_recv()
     for n in (0, 3, 4, 5):
@@ -217,7 +243,10 @@
     trace_ids = jnp.concatenate([tids[0], tids[1]], axis=1).astype(F32)
 
     lane = lax.broadcasted_iota(jnp.int32, (1, NZ, 1, 128), 3)
-    owner = lax.broadcasted_iota(jnp.int32, (1, NZ, 1, 128), 1)
+    slot = lax.broadcasted_iota(jnp.int32, (1, NZ, 1, 128), 1)
+    owner = jnp.zeros((1, NZ, 1, 128), jnp.int32)
+    for n, up in enumerate(UP):
+        owner = jnp.where(slot == n, (z + up) % NZ, owner)
     pick = jnp.where(lane == 2 * owner, 16.0, jnp.where(lane == 2 * owner + 1, 1.0, 0.0))
 
     def send_a1(j, i):
@@ -250,7 +279,7 @@
             source = sum_z.at[kind - 2, q]
         else:
             away = (1, -1, None, None, 3, -3, 4)[kind]
-            source = parts.at[q, :, (z + away) % NZ, :, C0:C1]
+            source = parts.at[q, :, SLOT[away % NZ], :, C0:C1]
         step = (1, -1, 2, -2, 1, -1, half)[kind]
         return remote(source, recv_c1.at[kind, q], rsc, j * 7 + kind, on_z(step))
 
@@ -260,38 +289,40 @@
             send_c1(j, kind).wait_recv()
         upper = jnp.where(j < 2, 1.0, 0.0)
         middle = recv_c1[6, q].astype(F32)
-        total = parts[q, :, (z + 2) % NZ, :, C0:C1].astype(F32) + recv_c1[4, q].astype(F32) + upper * middle
+        total = parts[q, :, SLOT[2], :, C0:C1].astype(F32) + recv_c1[4, q].astype(F32) + upper * middle
         sum_z[0, q] = total.astype(BF16)
-        total = parts[q, :, (z + 6) % NZ, :, C0:C1].astype(F32) + recv_c1[5, q].astype(F32) + (1.0 - upper) * middle
+        total = parts[q, :, SLOT[6], :, C0:C1].astype(F32) + recv_c1[5, q].astype(F32) + (1.0 - upper) * middle
         sum_z[1, q] = total.astype(BF16)
         send_c1(j, 2).start()
         send_c1(j, 3).start()
 
     def block_at(step):
-        return step + (step // 2) * (5 - 2 * step)
+        return (step % 2) * 2 + step // 2
 
     @pl.loop(0, NY)
     def _(step):
         j = block_at(step)
         q = (y - j) % NY
 
-        @pl.when(j == 1)
-        def _():
-            gather_a(2, 0, 1).wait_recv()
-            gather_a(3, 0, 1).wait_recv()
-
-        @pl.when(j == 3)
-        def _():
-            gather_a(0, 1, 1).wait_recv()
-            gather_a(1, 1, 1).wait_recv()
-
-        @pl.when(j == 2)
-        def _():
-            for i in range(NX):
-                gather_a(i, i // 2, 2).wait_recv()
-
-        gather_b(j, 1 - j // 2, 1).wait_recv()
-        gather_b(j, j // 2, 2).wait_recv()
+        for half in (0, 1):
+
+            @pl.when(j == 1)
+            def _():
+                gather_a(2, 0, 1, half).wait_recv()
+                gather_a(3, 0, 1, half).wait_recv()
+
+            @pl.when(j == 3)
+            def _():
+                gather_a(0, 1, 1, half).wait_recv()
+                gather_a(1, 1, 1, half).wait_recv()
+
+            @pl.when(j == 2)
+            def _():
+                for i in range(NX):
+                    gather_a(i, i // 2, 2, half).wait_recv()
+
+            gather_b(j, 1 - j // 2, 1, half).wait_recv()
+            gather_b(j, j // 2, 2, half).wait_recv()
         for kind in (0, 1, 4, 5, 6):
             gather_c(j, kind).wait_recv()
         at = pl.multiple_of(q * SPAN, SPAN)
@@ -333,27 +364,31 @@
 
             @pl.when(step == 3)
             def _():
-                send_b2(1).start()
-
-    relay_b(3)
-    send_b2(3).start()
-    relay_c(3)
+                send_b2(2).start()
+
+    relay_b(1)
+    send_b2(1).start()
+    relay_c(1)
 
     def trace_rows(first):
         return lax.dot_general(
             slopes[:, first : first + 256], flat[...], (((0,), (0,)), ((), ())), preferred_element_type=F32
         )
 
-    for n in range(2):
-        tg_send[n * 256 : n * 256 + 256, :] = trace_rows(ROWS + n * 256)
-    d3 = remote(tg_send, tg_recv, dd, 2, other)
-    d3.start()
-
-    relay_b(2)
-    send_b2(2).start()
-    relay_c(2)
+    def trace_to_other(n):
+        rows = pl.ds(n * 256, 256)
+        tg_send[rows, :] = trace_rows(ROWS + n * 256)
+        copy = remote(tg_send.at[rows], tg_recv.at[rows], dd, 2 + n, other)
+        copy.start()
+        return copy
+
+    d3 = [trace_to_other(0)]
+
+    relay_b(3)
+    send_b2(3).start()
     a2 = []
-    for i in (2, 1, 3, 0):
+
+    def sum_up_a(i):
         for j in near:
             send_a1(j, i).wait_recv()
         total = parts[y, (x + i) % NX, :, :, A0:A1].astype(F32)
@@ -363,20 +398,13 @@
         if i:
             a2.append(remote(sum_a.at[i], recv_a2.at[i - 1], rs, 26 + i, on_x(i)))
             a2[-1].start()
-    for j in range(NY):
-        for kind in range(4):
-            send_c1(j, kind).wait_recv()
-    for i in range(NY):
-        total = parts[i, :, z, :, C0:C1].astype(F32)
-        for kind in range(4):
-            total = total + recv_c1[kind, i].astype(F32)
-        sum_c[i] = total.astype(BF16)
-    c2 = []
-    for j, i in in_plane:
-        c2.append(
-            remote(sum_c.at[(y + j) % NY, (x + i) % NX], recv_c2.at[j * 4 + i], rsp, j * 4 + i, on_plane(j, i))
-        )
-        c2[-1].start()
+
+    sum_up_a(2)
+    relay_c(3)
+    sum_up_a(1)
+    sum_up_a(3)
+    d3.append(trace_to_other(1))
+    sum_up_a(0)
 
     for j in near:
         send_b2(j).wait_recv()
@@ -392,28 +420,31 @@
     sum_ab[:, :, A0:A1] = total.astype(BF16)
     ab3 = []
     for k in near_z:
-        ab3.append(remote(sum_ab.at[(z + k) % NZ], recv_ab3.at[k - 1], rs, 29 + k, on_z(k)))
+        ab3.append(remote(sum_ab.at[SLOT[k]], recv_ab3.at[k - 1], rs, 29 + k, on_z(k)))
         ab3[-1].start()
+
+    for j in range(NY):
+        for kind in range(4):
+            send_c1(j, kind).wait_recv()
+    for i in range(NY):
+        total = parts[i, :, 0, :, C0:C1].astype(F32)
+        for kind in range(4):
+            total = total + recv_c1[kind, i].astype(F32)
+        sum_c[i] = total.astype(BF16)
+    c2 = []
+    for j, i in in_plane:
+        c2.append(
+            remote(sum_c.at[(y + j) % NY, (x + i) % NX], recv_c2.at[j * 4 + i], rsp, j * 4 + i, on_plane(j, i))
+        )
+        c2[-1].start()
 
     for n in range(2):
         tg_own[n * 256 : n * 256 + 256, :] = trace_rows(n * 256)
-    d3.wait()
+    for copy in d3:
+        copy.wait_recv()
     trace_out[...] = (tg_own[...] + tg_recv[...]).astype(BF16)
 
-    for copy in c2:
-        copy.wait_recv()
-    total = sum_c[y, x].astype(F32)
-    for j, i in in_plane:
-        total = total + recv_c2[j * 4 + i].astype(F32)
-    code_out[:, C0:C1] = total.astype(BF16)
-    for copy in ab3:
-        copy.wait_recv()
-    total = sum_ab[z].astype(F32)
-    for k in range(NZ - 1):
-        total = total + recv_ab3[k].astype(F32)
-    code_out[:, A0:B1] = total.astype(BF16)
-
-    for copy in sent + c2 + a2 + ab3:
+    for copy in sent + a2 + d3:
         copy.wait_send()
     for j in range(NY):
         if j:
@@ -424,6 +455,22 @@
             send_b1(j, k).wait_send()
         for kind in range(7):
             send_c1(j, kind).wait_send()
+
+    for copy in c2:
+        copy.wait_recv()
+    total = sum_c[y, x].astype(F32)
+    for j, i in in_plane:
+        total = total + recv_c2[j * 4 + i].astype(F32)
+    code_out[:, C0:C1] = total.astype(BF16)
+    for copy in ab3:
+        copy.wait_recv()
+    total = sum_ab[0].astype(F32)
+    for k in range(NZ - 1):
+        total = total + recv_ab3[k].astype(F32)
+    code_out[:, A0:B1] = total.astype(BF16)
+
+    for copy in c2 + ab3:
+        copy.wait_send()
 
 
 def per_device(trace_emb, code_emb, trace_ids, code_ids, log_scale, bias):
@@ -457,18 +504,20 @@
         pltpu.VMEM((ROWS, WIDTH), F32),
         pltpu.VMEM((ROWS, WIDTH), F32),
         dma((6,)),
-        dma((3,)),
-        dma((3,)),
+        dma((4,)),
+        dma((4,)),
         dma((25,)),
         dma((25,)),
-        dma((16,)),
-        dma((16,)),
-        dma((16,)),
-        dma((16,)),
+        dma((32,)),
+        dma((32,)),
+        dma((32,)),
+        dma((32,)),
         dma((28,)),
         dma((28,)),
         dma((16,)),
         dma((16,)),
+        dma((12,)),
+        dma((12,)),
         dma((41,)),
         dma((41,)),
         dma((28,)),

time: 56.3 us -> 55.5 us (0.986)
  Pallas kernels: 52.3 us -> 50.9 us
    pallas_call x1, Pallas kernels: 52.3 us -> 50.9 us  [per_device(): pl.pallas_call(kernel, out_shape=(pltpu.VMEM((ROWS, WIDTH), BF16), pltpu....]
where the time goes in v5:
time: 55.5 us; the launch traced here: 54.5 us
  Pallas kernels  50.9 us (92%)
  between operations  1.93 us (3%)
  local copies, waits for them, and re-layouts  1.62 us (3%)
    pallas_call x1, Pallas kernels, per_device(): pl.pallas_call(kernel, out_shape=(pltpu.VMEM((ROWS, WIDTH), BF16), pltpu....  50.9 us
    unnamed x2, local copies, waits for them, and re-layouts  1.62 us

profile of v5, /device:TPU:16, one launch (start us, length us, event | category | flops | bytes accessed | tf_op | source)
XLA Modules:
  0.0 54.5 jit_solution(13267341392966281661)
XLA Ops:
  1.9 50.9 %contrast.1 = (bf16[512,1152]{1,0:T(8,128)(2,1)S(1)}, bf16[8,1152]{1,0:T(8,128)(2,1)S(1)}) custom-call(bf16[512,1152]{1,0:T(8,128)(2,1)} %trace_ref.1, bf16[8,1152]{1,0:T(8,128)(2,1)} %code_ref.1, s32[1,512]{1,0:T(1,128)} %bitcast.6, s32[1,8]{1,0:T(1,128)} %bitcast.7, f32[1,1]{1,0:T(1,128)} %bitcast.4.scale_ref, f32[1,1]{1,0:T(1,128)} %bitcast.5.shift_ref), custom_call_target="tpu_custom_call" | custom-call | tf_op jit(solution)/shard_map/contrast/pallas_call | solution.py:528
  52.9 1.0 %copy.10 = bf16[512,1152]{1,0:T(8,128)(2,1)} copy(bf16[512,1152]{1,0:T(8,128)(2,1)S(1)} %get-tuple-element.2) | data formatting | bytes 2359296
  53.9 0.6 %copy.11 = bf16[8,1152]{1,0:T(8,128)(2,1)} copy(bf16[8,1152]{1,0:T(8,128)(2,1)S(1)} %get-tuple-element.3) | data formatting | bytes 36864

commit v6 on v5

--- a/solution.py
+++ b/solution.py
@@ -87,8 +87,6 @@
         (tid_ref, tids.at[0]), (scale_ref, scale_v), (shift_ref, shift_v),
     )
     fetch = [pltpu.make_async_copy(src, dst, local.at[n]) for n, (src, dst) in enumerate(pairs)]
-    for n in (1, 2, 0, 3, 4, 5):
-        fetch[n].start()
 
     barrier = pltpu.get_barrier_semaphore()
     in_plane = [(j, i) for j in (0, 1, 3, 2) for i in (0, 1, 3, 2) if (j, i) != (0, 0)]
@@ -96,6 +94,8 @@
     partners += [on_z(k) for k in range(1, NZ)] + [other]
     for partner in partners:
         pl.semaphore_signal(barrier, inc=1, device_id=partner, device_id_type=MESH)
+    for n in (1, 2, 0, 3, 4, 5):
+        fetch[n].start()
 
     fetch[1].wait()
     fetch[2].wait()
@@ -209,10 +209,10 @@
     marks[y, x] = jnp.sum(codes[y, x, :, :, GM].astype(F32), axis=0).astype(BF16)
     ref = marks.at[y, x]
     m2 = [go(remote(ref, ref, ag, 18 + k, on_x(k))) for k in near]
+    pass_on(0, 0)
     set_out_both(1, 0)
     set_out_both(3, 0)
     pass_on_c(0)
-    pass_on(0, 0)
     set_out_both(2, 0)
     set_out_both(1, 1)
     set_out_both(3, 1)

time: 55.5 us -> 55.4 us (level)
  no operation moved by 1% of the time
where the time goes in v6:
time: 55.4 us; the launch traced here: 54.5 us
  Pallas kernels  51 us (92%)
  between operations  1.93 us (3%)
  local copies, waits for them, and re-layouts  1.62 us (3%)
    pallas_call x1, Pallas kernels, per_device(): pl.pallas_call(kernel, out_shape=(pltpu.VMEM((ROWS, WIDTH), BF16), pltpu....  51 us
    unnamed x2, local copies, waits for them, and re-layouts  1.62 us

profile of v6, /device:TPU:16, one launch (start us, length us, event | category | flops | bytes accessed | tf_op | source)
XLA Modules:
  0.0 54.5 jit_solution(1100119918699948306)
XLA Ops:
  1.9 51.0 %contrast.1 = (bf16[512,1152]{1,0:T(8,128)(2,1)S(1)}, bf16[8,1152]{1,0:T(8,128)(2,1)S(1)}) custom-call(bf16[512,1152]{1,0:T(8,128)(2,1)} %trace_ref.1, bf16[8,1152]{1,0:T(8,128)(2,1)} %code_ref.1, s32[1,512]{1,0:T(1,128)} %bitcast.6, s32[1,8]{1,0:T(1,128)} %bitcast.7, f32[1,1]{1,0:T(1,128)} %bitcast.4.scale_ref, f32[1,1]{1,0:T(1,128)} %bitcast.5.shift_ref), custom_call_target="tpu_custom_call" | custom-call | tf_op jit(solution)/shard_map/contrast/pallas_call | solution.py:528
  52.9 1.0 %copy.10 = bf16[512,1152]{1,0:T(8,128)(2,1)} copy(bf16[512,1152]{1,0:T(8,128)(2,1)S(1)} %get-tuple-element.2) | data formatting | bytes 2359296
  53.9 0.6 %copy.11 = bf16[8,1152]{1,0:T(8,128)(2,1)} copy(bf16[8,1152]{1,0:T(8,128)(2,1)S(1)} %get-tuple-element.3) | data formatting | bytes 36864
